TPU v7x, 32 devices: a whole 2x2x4 slice. The times are simulated.
32 devices in a mesh: ctx: 8 (over y, x, core), ep: 4 (over z).
Axes of the slice: x: 2, y: 2, z: 4, core: 2. Of those that a mesh axis runs over, the one named last changes fastest.
Arguments:
- queries: bfloat16 [2048, 128, 192], P('ctx', 'ep'), may hold values from -7 to 7
- latents: bfloat16 [2048, 576], P('ctx'), may hold values from -7 to 7
- key_absorb: bfloat16 [128, 128, 512], P('ep'), may hold values from -0.5 to 0.5
- value_absorb: bfloat16 [128, 512, 128], P('ep'), may hold values from -1.5 to 1.5
- out_proj: bfloat16 [16384, 7168], P(None, 'ctx'), may hold values from -0.046875 to 0.046875
- residual_in: bfloat16 [2048, 7168], P(('ctx', 'ep')), may hold values from -3 to 3
- norm_gain: float32 [7168], replicated, may hold values from 0.1 to 1.9
- expert_gate: bfloat16 [4, 7168, 2048], P('ep', None, 'ctx'), may hold values from -0.0625 to 0.0625
- expert_up: bfloat16 [4, 7168, 2048], P('ep', None, 'ctx'), may hold values from -0.0625 to 0.0625
- expert_down: bfloat16 [4, 2048, 7168], P('ep', 'ctx'), may hold values from -0.125 to 0.125
- route_ids: int32 [2048, 8], P(('ctx', 'ep')), may hold values from 0 to 255, as said below
- route_weights: float32 [2048, 8], P(('ctx', 'ep')), may hold values from 0.5 to 1.5
Outputs:
- layer_out: bfloat16 [2048, 7168], P(('ctx', 'ep'))
Inputs may be any that keep to these rules, and one draw needn't show every extreme that they name: `route_ids`: each row names 8 different experts. In every aligned block of 64 rows (the rows of one device) each expert below 4 is named by at most 2 rows, and some expert by exactly 2.
All inputs are finite; a program needn't handle non-finite values.
Results may differ from a plain program's by a relative error of at most 0.028.
Values may be sent and summed in bfloat16 or wider, within the bound.
A program may use at most 320 MiB of HBM per device.

v0:
```python
import jax
import jax.numpy as jnp
from jax import lax
from jax.sharding import PartitionSpec as P

NOPE = 128
ROPE = 64
LATENT = 512
TOPK = 8
CAP = 2


def attend_block(state, query_full, keys, key_start, query_start):
    running_max, running_sum, numerator = state
    scale = (NOPE + ROPE) ** (-0.5)
    scores = jnp.einsum("thc,sc->hts", query_full, keys, preferred_element_type=jnp.float32) * scale
    query_pos = query_start + jnp.arange(query_full.shape[0], dtype=jnp.int32)
    key_pos = key_start + jnp.arange(keys.shape[0], dtype=jnp.int32)
    allowed = (query_pos[:, None] >= key_pos[None, :])[None]
    scores = jnp.where(allowed, scores, -1e30)
    new_max = jnp.maximum(running_max, jnp.max(scores, axis=2))
    weights = jnp.where(allowed, jnp.exp(scores - new_max[:, :, None]), 0.0)
    factor = jnp.exp(running_max - new_max)
    running_sum = running_sum * factor + jnp.sum(weights, axis=2)
    values = jnp.einsum(
        "hts,sc->htc",
        weights.astype(jnp.bfloat16),
        keys[:, :LATENT],
        preferred_element_type=jnp.float32,
    )
    numerator = numerator * factor[:, :, None] + values
    return (new_max, running_sum, numerator)


def on_device(
    queries,
    latents,
    key_absorb,
    value_absorb,
    out_proj,
    residual_in,
    norm_gain,
    expert_gate,
    expert_up,
    expert_down,
    route_ids,
    route_weights,
):
    rows = queries.shape[0]
    local_heads = queries.shape[1]
    query_start = lax.axis_index("ctx") * rows
    absorbed = jnp.einsum(
        "thn,hnc->thc", queries[:, :, :NOPE], key_absorb, preferred_element_type=jnp.float32
    ).astype(jnp.bfloat16)
    query_full = jnp.concatenate([absorbed, queries[:, :, NOPE:]], axis=2)
    initial = (
        jnp.full((local_heads, rows), -1e30, jnp.float32),
        jnp.zeros((local_heads, rows), jnp.float32),
        jnp.zeros((local_heads, rows, LATENT), jnp.float32),
    )
    piece = lax.all_gather(latents, "ctx", axis=0, tiled=True)
    start = jnp.int32(0)

    def compute(inner):
        for begin in range(0, piece.shape[0], 512):
            finish = min(begin + 512, piece.shape[0])
            inner = attend_block(inner, query_full, piece[begin:finish], start + begin, query_start)
        return inner

    def unchanged(inner):
        return inner

    running_max, running_sum, numerator = lax.cond(
        start <= query_start + rows - 1, compute, unchanged, initial
    )
    mixed = (numerator / running_sum[:, :, None]).astype(jnp.bfloat16)
    head_out = jnp.einsum(
        "htc,hcv->thv", mixed, value_absorb, preferred_element_type=jnp.float32
    ).astype(jnp.bfloat16)
    head_rows = head_out.reshape(rows, -1)
    columns = out_proj.shape[1]
    ctx_count = lax.axis_size("ctx")
    regrouped = lax.all_to_all(head_rows, "ep", split_axis=0, concat_axis=1, tiled=True)
    complete = jnp.dot(
        lax.all_gather(regrouped, "ctx", axis=0, tiled=True),
        out_proj,
        preferred_element_type=jnp.float32,
    ).astype(jnp.bfloat16)
    complete = complete.reshape(ctx_count, -1, columns)
    attended = lax.all_to_all(complete, "ctx", split_axis=0, concat_axis=2, tiled=True).reshape(
        -1, columns * ctx_count
    )
    wide = residual_in.astype(jnp.float32) + attended.astype(jnp.float32)
    hidden = wide.astype(jnp.bfloat16)
    hidden_wide = hidden.astype(jnp.float32)
    square = jnp.mean(hidden_wide * hidden_wide, axis=1, keepdims=True)
    normed = (hidden_wide * lax.rsqrt(square + 1e-06) * norm_gain).astype(jnp.bfloat16)
    tokens_here = hidden.shape[0]
    window = lax.axis_size("ep")
    flat_ids = route_ids.reshape(-1)
    chosen = (flat_ids[:, None] == jnp.arange(window, dtype=jnp.int32)[None, :]).astype(jnp.int32)
    earlier = jnp.cumsum(chosen, axis=0) - chosen
    slot = jnp.sum(earlier * chosen, axis=1)
    place = chosen[:, :, None] * (
        slot[:, None, None] == jnp.arange(CAP, dtype=jnp.int32)[None, None, :]
    ).astype(jnp.int32)
    place = place.reshape(tokens_here, TOPK, window * CAP).astype(jnp.float32)
    gather_table = jnp.sum(place, axis=1).astype(jnp.bfloat16)
    combine_table = jnp.sum(place * route_weights[:, :, None], axis=1)
    outgoing = lax.dot_general(
        gather_table, normed, (((0,), (0,)), ((), ())), preferred_element_type=jnp.float32
    ).astype(jnp.bfloat16)
    outgoing = outgoing.reshape(window, CAP, -1)
    arrived = lax.all_to_all(outgoing, "ep", split_axis=0, concat_axis=0, tiled=True)
    gate_weight = expert_gate[0]
    up_weight = expert_up[0]
    down_weight = expert_down[0]

    def expert_piece(piece):
        flat_rows = piece.reshape(-1, piece.shape[2])
        gate = jnp.dot(flat_rows, gate_weight, preferred_element_type=jnp.float32)
        upper = jnp.dot(flat_rows, up_weight, preferred_element_type=jnp.float32)
        activated = (jax.nn.silu(gate) * upper).astype(jnp.bfloat16)
        return jnp.dot(activated, down_weight, preferred_element_type=jnp.float32).reshape(
            piece.shape[0], piece.shape[1], -1
        )

    partial_out = expert_piece(lax.all_gather(arrived, "ctx", axis=0, tiled=True))
    result = lax.psum_scatter(
        partial_out.astype(jnp.bfloat16), "ctx", scatter_dimension=0, tiled=True
    )
    returned = lax.all_to_all(result, "ep", split_axis=0, concat_axis=0, tiled=True)
    mixture = jnp.dot(
        combine_table,
        returned.reshape(window * CAP, -1).astype(jnp.float32),
        precision=lax.Precision.HIGHEST,
    )
    return (hidden_wide + mixture).astype(jnp.bfloat16)


def solution(mesh):
    placed = (
        P("ctx", "ep", None),
        P("ctx", None),
        P("ep", None, None),
        P("ep", None, None),
        P(None, "ctx"),
        P(("ctx", "ep"), None),
        P(),
        P("ep", None, "ctx"),
        P("ep", None, "ctx"),
        P("ep", "ctx", None),
        P(("ctx", "ep"), None),
        P(("ctx", "ep"), None),
    )
    return jax.shard_map(
        on_device, mesh=mesh, in_specs=placed, out_specs=P(("ctx", "ep"), None), check_vma=False
    )
```

profile of v0, /device:TPU:0, one launch (start us, length us, event | category | flops | bytes accessed | tf_op | source)
XLA Modules:
  0.0 502.1 jit_solution(1379178117397721346)
XLA Ops:
  6.5 0.0 all-gather.3.cloned.1.call-start
  6.5 0.7 all-gather.3.cloned.1.call-update
  7.3 0.0 all-gather.5.cloned.1.call-start
  7.3 5.3 %convert_bitcast_fusion = bf16[256,32,512]{0,2,1:T(8,128)(2,1)S(1)} fusion(bf16[32,128,512]{2,1,0:T(8,128)(2,1)} %param.16, bf16[256,32,192]{0,2,1:T(8,128)(2,1)} %param.14), kind=kOutput, calls=%fused_computation.89 | convolution fusion | flops 1077936128 | bytes 14680064 | tf_op jit(solution)/shard_map/thn,hnc->thc/dot_general | solution.py:52
  12.6 0.0 slice-done.3
  12.6 4.1 pad_maximum_fusion
  16.7 24.6 %all-gather.3.cloned.1.call-done = bf16[2048,576]{0,1:T(8,128)(2,1)} async-done(((bf16[256,576]{0,1:T(8,128)(2,1)}), bf16[2048,576]{0,1:T(8,128)(2,1)}) %all-gather.3.cloned.1.call-update) | async-done | bytes 2359312 | tf_op jit(solution)/shard_map/all_gather | solution.py:61
  41.3 157.2 %conditional.1 = (f32[32,256]{1,0:T(8,128)S(1)}, f32[32,256,512]{2,1,0:T(8,128)}) conditional(s32[]{:T(128)} %convert_element_type.99, () %tuple.13, (s32[]{:T(128)}, bf16[2048,576]{0,1:T(8,128)(2,1)}, bf16[256,32,576]{0,2,1:T(8,128)(2,1)}) %tuple.14), branch_computations={%region_0.0_spmd, %region_1.10_spmd} | conditional | flops 36755300352 | bytes 474003584 | solution.py:73
  41.3 0.4 iota_compare_fusion
  41.7 0.0 slice-start
  41.7 4.4 copy.45
  46.2 10.3 %fusion = (f32[32,256]{1,0:T(8,128)S(1)}, f32[512,256,32]{1,0,2:T(8,128)S(1)}) fusion(pred[256,512]{0,1:T(8,128)(4,1)S(1)} %get-tuple-element.31, bf16[256,32,576]{0,2,1:T(8,128)(2,1)} %get-tuple-element.13, bf16[2048,576]{0,1:T(8,128)(2,1)} %get-tuple-element.12), kind=kOutput, calls=%fused_computation.9 | convolution fusion | flops 4844412928 | bytes 26968064 | tf_op jit(solution)/shard_map/cond/branch_1_fun/thc,sc->hts/dot_general | solution.py:16
  56.5 12.3 %fusion.1 = (f32[32,256]{1,0:T(8,128)S(1)}, f32[512,256,32]{1,0,2:T(8,128)}) fusion(pred[256,512]{0,1:T(8,128)(4,1)S(1)} %get-tuple-element.32, bf16[256,32,576]{0,2,1:T(8,128)(2,1)S(1)} %bitcast.148, bf16[2048,576]{0,1:T(8,128)(2,1)} %get-tuple-element.12), kind=kOutput, calls=%fused_computation.10 | convolution fusion | flops 4844412928 | bytes 26968064 | tf_op jit(solution)/shard_map/cond/branch_1_fun/thc,sc->hts/dot_general | solution.py:16
  68.8 11.9 %fusion.2 = (f32[32,256]{1,0:T(8,128)S(1)}, f32[512,256,32]{1,0,2:T(8,128)}) fusion(pred[256,512]{0,1:T(8,128)(4,1)S(1)} %get-tuple-element.33, bf16[256,32,576]{0,2,1:T(8,128)(2,1)S(1)} %bitcast.148, bf16[2048,576]{0,1:T(8,128)(2,1)} %get-tuple-element.12), kind=kOutput, calls=%fused_computation.11 | convolution fusion | flops 4844412928 | bytes 26968064 | tf_op jit(solution)/shard_map/cond/branch_1_fun/thc,sc->hts/dot_general | solution.py:16
  80.7 12.3 %fusion.3 = (f32[32,256]{1,0:T(8,128)S(1)}, f32[512,256,32]{1,0,2:T(8,128)}) fusion(pred[256,512]{0,1:T(8,128)(4,1)S(1)} %get-tuple-element.34, bf16[256,32,576]{0,2,1:T(8,128)(2,1)S(1)} %bitcast.148, bf16[2048,576]{0,1:T(8,128)(2,1)} %get-tuple-element.12), kind=kOutput, calls=%fused_computation.12 | convolution fusion | flops 4844412928 | bytes 26968064 | tf_op jit(solution)/shard_map/cond/branch_1_fun/thc,sc->hts/dot_general | solution.py:16
  93.0 0.0 copy-done
  93.0 0.0 copy-start.1
  93.0 11.9 %fusion.5 = (f32[32,256]{1,0:T(8,128)S(1)}, f32[32,256]{1,0:T(8,128)S(1)}) fusion(f32[512,256,32]{1,0,2:T(8,128)S(1)} %get-tuple-element.42, f32[32,256]{1,0:T(8,128)S(1)} %get-tuple-element.30, pred[256,512]{0,1:T(8,128)(4,1)S(1)} %get-tuple-element.31, f32[32,256]{1,0:T(8,128)S(1)} %get-tuple-element.26, f32[512,256,32]{1,0,2:T(8,128)} %get-tuple-element.40, ...), kind=kLoop, calls=%fused_computation.14 | loop fusion | flops 41926656 | bytes 33947648 | tf_op jit(solution)/shard_map/cond/branch_1_fun/reduce_sum | solution.py:24
  105.0 16.6 %fusion.17 = f32[32,256,512]{2,1,0:T(8,128)} fusion(f32[512,256,32]{1,0,2:T(8,128)} %copy-done, f32[32,256]{1,0:T(8,128)S(1)} %get-tuple-element.30, pred[256,512]{0,1:T(8,128)(4,1)S(1)} %get-tuple-element.31, bf16[2048,576]{1,0:T(8,128)(2,1)S(1)} %copy-done.1), kind=kOutput, calls=%fused_computation.23 | convolution fusion | flops 4315938816 | bytes 34242560 | tf_op jit(solution)/shard_map/cond/branch_1_fun/hts,sc->htc/dot_general | solution.py:25
  121.5 16.6 %fusion.15 = f32[32,256,512]{2,1,0:T(8,128)} fusion(f32[512,256,32]{1,0,2:T(8,128)} %get-tuple-element.40, f32[32,256]{1,0:T(8,128)S(1)} %get-tuple-element.26, pred[256,512]{0,1:T(8,128)(4,1)S(1)} %get-tuple-element.32, bf16[2048,576]{1,0:T(8,128)(2,1)S(1)} %copy-done.1), kind=kOutput, calls=%fused_computation.22 | convolution fusion | flops 4315938816 | bytes 34242560 | tf_op jit(solution)/shard_map/cond/branch_1_fun/hts,sc->htc/dot_general | solution.py:25
  138.2 14.4 %fusion.9 = (f32[32,256]{1,0:T(8,128)S(1)}, f32[32,256]{1,0:T(8,128)S(1)}) fusion(f32[512,256,32]{1,0,2:T(8,128)} %get-tuple-element.38, f32[32,256]{1,0:T(8,128)S(1)} %get-tuple-element.25, pred[256,512]{0,1:T(8,128)(4,1)S(1)} %get-tuple-element.33, f32[32,256]{1,0:T(8,128)S(1)} %get-tuple-element.24, f32[512,256,32]{1,0,2:T(8,128)} %get-tuple-element.36, ...), kind=kLoop, calls=%fused_computation.18 | loop fusion | flops 41926656 | bytes 33947648 | tf_op jit(solution)/shard_map/cond/branch_1_fun/reduce_sum | solution.py:24
  152.6 16.6 %fusion.13 = f32[32,256,512]{2,1,0:T(8,128)} fusion(f32[512,256,32]{1,0,2:T(8,128)} %get-tuple-element.38, f32[32,256]{1,0:T(8,128)S(1)} %get-tuple-element.25, pred[256,512]{0,1:T(8,128)(4,1)S(1)} %get-tuple-element.33, bf16[2048,576]{1,0:T(8,128)(2,1)S(1)} %copy-done.1), kind=kOutput, calls=%fused_computation.21 | convolution fusion | flops 4315938816 | bytes 34242560 | tf_op jit(solution)/shard_map/cond/branch_1_fun/hts,sc->htc/dot_general | solution.py:25
  169.2 29.3 %multiply_add_fusion = f32[32,256,512]{2,1,0:T(8,128)} fusion(f32[32,256,512]{2,1,0:T(8,128)} %fusion.13, f32[32,256,512]{2,1,0:T(8,128)} %fusion.15, f32[32,256,512]{2,1,0:T(8,128)} %fusion.17, f32[512,256,32]{1,0,2:T(8,128)} %get-tuple-element.36, f32[32,256]{1,0:T(8,128)S(1)} %get-tuple-element.23, f32[32,256]{1,0:T(8,128)S(1)} %get-tuple-element.22, ...), kind=kOutput, calls=%fused_computation.4 | convolution fusion | flops 4345298944 | bytes 84705280 | tf_op jit(solution)/shard_map/cond/branch_1_fun/hts,sc->htc/dot_general | solution.py:25
  198.5 8.5 %convert_bitcast_fusion.1 = bf16[256,32,128]{2,0,1:T(8,128)(2,1)S(1)} fusion(bf16[32,512,128]{2,1,0:T(8,128)(2,1)} %param.17, f32[32,256,512]{2,1,0:T(8,128)} %get-tuple-element.16, f32[32,256]{1,0:T(8,128)S(1)} %get-tuple-element.17), kind=kOutput, calls=%fused_computation.102 | convolution fusion | flops 1083179008 | bytes 23101440 | tf_op jit(solution)/shard_map/htc,hcv->thv/dot_general | solution.py:77
  207.0 0.0 copy-start.2
  207.0 1.4 copy.55
  208.4 2.3 all_to_all.27
  210.7 53.2 %all_to_all.38 = bf16[4,64,4096]{2,1,0:T(8,128)(2,1)S(1)} all-to-all(bf16[4,64,4096]{2,1,0:T(8,128)(2,1)} %all_to_all.27), channel_id=1, replica_groups=mesh['ctx'=8,'ep'=4] {'ep'}, dimensions={0} | all-to-all | bytes 4194304 | tf_op jit(solution)/shard_map/all_to_all | solution.py:83
  263.9 1.5 copy.71
  265.4 0.0 all-gather.5.cloned.1.call-update
  265.4 0.1 copy.58
  265.5 0.1 eq.47
  265.6 0.1 eq.51
  265.7 1.2 reduce-window.6
  266.9 0.2 slice_reduce_fusion
  267.2 0.2 reduce-window.9
  267.4 0.1 add_bitcast_fusion
  267.4 86.2 %all-gather.5.cloned.1.call-done = bf16[512,16384]{1,0:T(8,128)(2,1)} async-done(((bf16[64,16384]{1,0:T(8,128)(2,1)}), bf16[512,16384]{1,0:T(8,128)(2,1)}) %all-gather.5.cloned.1.call-update) | async-done | bytes 16777232 | tf_op jit(solution)/shard_map/all_gather | solution.py:85
  353.6 24.7 %convolution_convert_fusion.2 = bf16[512,896]{1,0:T(8,128)(2,1)} fusion(bf16[512,16384]{1,0:T(8,128)(2,1)} %all-gather.5.cloned.1.call-done, bf16[16384,896]{1,0:T(8,128)(2,1)} %param.18), kind=kOutput, calls=%fused_computation.109 | convolution fusion | flops 15032844288 | bytes 47054848 | tf_op jit(solution)/shard_map/dot_general | solution.py:84
  378.3 3.7 all-to-all-start.1
  382.0 0.0 all-reduce.3.cloned.1.call-start
  382.0 0.0 copy-done.3
  382.0 0.1 copy.60
  382.2 0.2 convert_element_type.116
  382.3 0.2 fusion.91
  382.5 13.3 %all-to-all-done.1 = bf16[8,64,896]{2,1,0:T(8,128)(2,1)S(1)} async-done(((bf16[8,64,896]{2,1,0:T(8,128)(2,1)}), bf16[8,64,896]{2,1,0:T(8,128)(2,1)S(1)}, u32[]{:S(2)}, u32[]{:S(2)}) %all-to-all-start.1) | async-done | bytes 917536 | tf_op jit(solution)/shard_map/all_to_all | solution.py:90
  395.9 0.1 fusion.94
  396.0 0.1 copy.72
  396.2 1.6 fusion.72
  397.8 0.4 convolution_convert_fusion.1
  398.2 0.1 reshape.275
  398.2 10.3 %all_to_all.39 = bf16[4,2,7168]{2,1,0:T(2,128)(2,1)S(1)} all-to-all(bf16[4,2,7168]{2,1,0:T(2,128)(2,1)S(1)} %reshape.275), channel_id=1, replica_groups=mesh['ctx'=8,'ep'=4] {'ep'}, dimensions={0} | all-to-all | bytes 229376 | tf_op jit(solution)/shard_map/all_to_all | solution.py:114
  408.5 9.7 %all_gather.11 = bf16[32,2,7168]{2,1,0:T(2,128)(2,1)S(1)} all-gather(bf16[4,2,7168]{2,1,0:T(2,128)(2,1)S(1)} %all_to_all.39), channel_id=1, replica_groups=mesh['ctx'=8,'ep'=4] {'ctx'}, dimensions={0}, use_global_device_ids=true | all-gather | bytes 1032192 | tf_op jit(solution)/shard_map/all_gather | solution.py:128
  418.2 0.3 reshape.276
  418.6 2.8 fusion.69
  421.3 2.8 fusion.78
  424.1 3.7 convolution_convert_fusion
  427.8 0.0 all-reduce.3.cloned.1.call-update
  427.9 0.6 dynamic-slice
  429.1 53.1 %all-reduce.3.cloned.1.call-done = bf16[32,2,7168]{2,0,1:T(8,128)(2,1)} async-done(((bf16[32,2,7168]{2,0,1:T(8,128)(2,1)}), bf16[32,2,7168]{2,0,1:T(8,128)(2,1)}) %all-reduce.3.cloned.1.call-update) | async-done | bytes 917520
  482.2 1.0 constant_dynamic-slice_fusion
  483.2 0.1 copy.62
  483.3 10.1 %all_to_all.40 = bf16[4,2,7168]{2,1,0:T(2,128)(2,1)S(1)} all-to-all(bf16[4,2,7168]{2,1,0:T(2,128)(2,1)S(1)} %copy.62), channel_id=1, replica_groups=mesh['ctx'=8,'ep'=4] {'ep'}, dimensions={0} | all-to-all | bytes 229376 | tf_op jit(solution)/shard_map/all_to_all | solution.py:132
  493.5 1.9 fusion.65
  (29 shorter events, 0.2 us)
Async XLA Ops:
  6.5 6.0 %slice-start.3 = ((bf16[256,32,192]{0,2,1:T(8,128)(2,1)}), bf16[256,32,64]{0,2,1:T(8,128)(2,1)S(1)}, s32[]{:S(2)}) async-start(bf16[256,32,192]{0,2,1:T(8,128)(2,1)} %param.14), calls=%async_computation.10 | async-start | bytes 2097152 | tf_op jit(solution)/shard_map/slice | solution.py:55
  6.5 34.8 %all-gather.3.cloned.1.call-start = ((), (), s32[]{:S(2)}) async-start(), calls=%async_computation.4 | async-start | bytes 2654208 | tf_op jit(solution)/shard_map/all_gather | solution.py:61
  7.3 346.3 %all-gather.5.cloned.1.call-start = ((), (), s32[]{:S(2)}) async-start(), calls=%async_computation.5 | async-start | bytes 18874368 | tf_op jit(solution)/shard_map/all_gather | solution.py:85
  41.7 14.8 %slice-start = ((s8[9437184]{0:T(1024)(128)(4,1)}), s8[1048576]{0:T(1024)(128)(4,1)S(1)}, s32[]{:S(2)}) async-start(s8[9437184]{0:T(1024)(128)(4,1)} %bitcast.147), calls=%async_computation.7 | async-start | bytes 2097152 | tf_op jit(solution)/shard_map/cond
  46.2 10.3 %slice-start.1 = ((s8[9437184]{0:T(1024)(128)(4,1)}), s8[4194304]{0:T(1024)(128)(4,1)S(1)}, s32[]{:S(2)}) async-start(s8[9437184]{0:T(1024)(128)(4,1)} %bitcast.147), calls=%async_computation.8 | async-start | bytes 8388608 | tf_op jit(solution)/shard_map/cond
  46.2 10.3 %slice-start.2 = ((s8[9437184]{0:T(1024)(128)(4,1)}), s8[4194304]{0:T(1024)(128)(4,1)S(1)}, s32[]{:S(2)}) async-start(s8[9437184]{0:T(1024)(128)(4,1)} %bitcast.147), calls=%async_computation.9 | async-start | bytes 8388608 | tf_op jit(solution)/shard_map/cond
  56.5 36.6 %copy-start = (f32[512,256,32]{1,0,2:T(8,128)}, f32[512,256,32]{1,0,2:T(8,128)S(1)}, u32[]{:S(2)}) copy-start(f32[512,256,32]{1,0,2:T(8,128)S(1)} %get-tuple-element.42) | copy-start | bytes 50331652 | tf_op jit(solution)/shard_map/cond
  93.0 11.9 %copy-start.1 = (bf16[2048,576]{1,0:T(8,128)(2,1)S(1)}, bf16[2048,576]{1,0:T(8,128)(2,1)}, u32[]{:S(2)}) copy-start(bf16[2048,576]{1,0:T(8,128)(2,1)} %copy.45) | copy-start | bytes 7077892 | tf_op jit(solution)/shard_map/cond
  207.0 58.4 %copy-start.2 = (s32[64,8]{0,1:T(8,128)S(1)}, s32[64,8]{0,1:T(8,128)}, u32[]{:S(2)}) copy-start(s32[64,8]{0,1:T(8,128)} %param.24) | copy-start | bytes 6148
  267.4 114.6 %copy-start.3 = (f32[64,8]{0,1:T(8,128)S(1)}, f32[64,8]{0,1:T(8,128)}, u32[]{:S(2)}) copy-start(f32[64,8]{0,1:T(8,128)} %param.25) | copy-start | bytes 6148
  267.4 130.3 %copy-start.4 = (f32[7168]{0:T(1024)S(1)}, f32[7168]{0:T(1024)}, u32[]{:S(2)}) copy-start(f32[7168]{0:T(1024)} %param.20) | copy-start | bytes 86020
  378.3 49.6 %copy-start.5 = (u32[32]{0:T(128)S(1)}, u32[32]{0:T(128)}, u32[]{:S(2)}) copy-start(u32[32]{0:T(128)} %constant.53) | copy-start | bytes 388
  378.3 17.6 %all-to-all-start.1 = ((bf16[8,64,896]{2,1,0:T(8,128)(2,1)}), bf16[8,64,896]{2,1,0:T(8,128)(2,1)S(1)}, u32[]{:S(2)}, u32[]{:S(2)}) async-start(bf16[8,64,896]{2,1,0:T(8,128)(2,1)} %bitcast.15), calls=%async_computation.1 | async-start | bytes 1835008 | tf_op jit(solution)/shard_map/all_to_all | solution.py:90
  382.0 100.2 %all-reduce.3.cloned.1.call-start = ((), (), s32[]{:S(2)}) async-start(), calls=%async_computation.6 | async-start | bytes 1835008
Sparse Core Ops, SparseCore 0:
  9.2 32.0 all-gather.2
  265.6 87.9 all-gather.4
  428.0 54.1 all-reduce.2
where the time goes:
time: 505 us; the launch traced here: 502 us
  waiting for transfers between devices  178 us (35%)
  matrix products  176 us (35%)
  blocking collectives  83.3 us (16%)
  other arithmetic  34.3 us (7%)
  between operations  14.1 us (3%)
  local copies, waits for them, and re-layouts  12.7 us (3%)
    all_gather x1, waiting for transfers between devices, on_device(): lax.all_gather(regrouped, 'ctx', axis=0, tiled=True)  86.2 us
    dot_general x4, matrix products, attend_block(): jnp.einsum('hts,sc->htc', weights.astype(jnp.bfloat16), keys[:, :LATENT],...  79.1 us
    unnamed x4, waiting for transfers between devices  53.8 us
    all_to_all x1, blocking collectives, on_device(): lax.all_to_all(head_rows, 'ep', split_axis=0, concat_axis=1, tiled=True)  53.2 us
    dot_general x4, matrix products, attend_block(): jnp.einsum('thc,sc->hts', query_full, keys, preferred_element_type=jnp.fl...  46.8 us
    reduce_sum x2, other arithmetic, attend_block(): running_sum = running_sum * factor + jnp.sum(weights, axis=2)  26.3 us
    dot_general x1, matrix products, on_device(): jnp.dot(lax.all_gather(regrouped, 'ctx', axis=0, tiled=True), out_proj, p...  24.7 us
    all_gather x1, waiting for transfers between devices, on_device(): piece = lax.all_gather(latents, 'ctx', axis=0, tiled=True)  24.6 us
  transfers between devices with their start and end apart: 4, of which 4 were waited for; matrix products, arithmetic and copies ran while one was open for 2% of the time, Pallas kernels for 0%

commit v1 on v0

v1 whole, which is shorter than its diff:
```python
import jax
import jax.numpy as jnp
from jax import lax
from jax.experimental import pallas as pl
from jax.experimental.pallas import tpu as pltpu
from jax.sharding import PartitionSpec as P

NOPE = 128
ROPE = 64
LATENT = 512
VHEAD = 128
TOPK = 8
CAP = 2
CHUNKS = 4
KEY_BLOCK = 512
LOG2E = 1.4426950408889634


def over_first(a, b):
    return lax.dot_general(a, b, (((0,), (0,)), ((), ())), preferred_element_type=jnp.float32)


def attention_kernel(start_ref, q_ref, ka_ref, va_ref, lat_ref, latt_ref, out_ref, qf_ref, s_ref):
    factor = (NOPE + ROPE) ** (-0.5) * LOG2E
    rows = q_ref.shape[2]
    keys = lat_ref.shape[0]
    query_start = start_ref[0]
    absorbed = over_first(ka_ref[0], q_ref[0, :NOPE, :])
    qf_ref[:LATENT, :] = (absorbed * factor).astype(jnp.bfloat16)
    qf_ref[LATENT:, :] = (q_ref[0, NOPE:, :].astype(jnp.float32) * factor).astype(jnp.bfloat16)
    ahead = lax.broadcasted_iota(jnp.int32, (KEY_BLOCK, rows), 0) - lax.broadcasted_iota(
        jnp.int32, (KEY_BLOCK, rows), 1
    )
    top = jnp.full((8, rows), -1e30, jnp.float32)
    for begin in range(0, keys, KEY_BLOCK):
        scores = jnp.dot(
            lat_ref[begin : begin + KEY_BLOCK, :], qf_ref[...], preferred_element_type=jnp.float32
        )
        scores = jnp.where(ahead <= query_start - begin, scores, -1e30)
        s_ref[begin : begin + KEY_BLOCK, :] = scores
        top = jnp.maximum(top, jnp.max(scores.reshape(KEY_BLOCK // 8, 8, rows), axis=0))
    top = jnp.max(top, axis=0, keepdims=True)
    total = jnp.zeros((8, rows), jnp.float32)
    mixed = jnp.zeros((LATENT, rows), jnp.float32)
    for begin in range(0, keys, KEY_BLOCK):
        weights = jnp.exp2(s_ref[begin : begin + KEY_BLOCK, :] - top)
        total = total + jnp.sum(weights.reshape(KEY_BLOCK // 8, 8, rows), axis=0)
        mixed = mixed + jnp.dot(
            latt_ref[:LATENT, begin : begin + KEY_BLOCK],
            weights.astype(jnp.bfloat16),
            preferred_element_type=jnp.float32,
        )
    inverse = 1.0 / jnp.sum(total, axis=0, keepdims=True)
    mixed = (mixed * inverse).astype(jnp.bfloat16)
    out_ref[...] = over_first(mixed, va_ref[0]).astype(jnp.bfloat16)


def attention(chunk, count, query_start, queries_t, key_absorb, value_absorb, keys, keys_t):
    rows = queries_t.shape[2]
    width = queries_t.shape[1]
    total, latent_width = keys.shape
    first = chunk * count

    def by_head(i, _):
        return (first + i, 0, 0)

    return pl.pallas_call(
        attention_kernel,
        grid_spec=pltpu.PrefetchScalarGridSpec(
            num_scalar_prefetch=1,
            grid=(count,),
            in_specs=[
                pl.BlockSpec((1, width, rows), by_head),
                pl.BlockSpec((1, NOPE, LATENT), by_head),
                pl.BlockSpec((1, LATENT, VHEAD), by_head),
                pl.BlockSpec((total, latent_width), lambda i, _: (0, 0)),
                pl.BlockSpec((latent_width, total), lambda i, _: (0, 0)),
            ],
            out_specs=pl.BlockSpec((rows, VHEAD), lambda i, _: (0, i)),
            scratch_shapes=[
                pltpu.VMEM((latent_width, rows), jnp.bfloat16),
                pltpu.VMEM((total, rows), jnp.float32),
            ],
        ),
        out_shape=jax.ShapeDtypeStruct((rows, count * VHEAD), jnp.bfloat16),
        compiler_params=pltpu.CompilerParams(vmem_limit_bytes=48 * 2 ** 20),
        cost_estimate=pl.CostEstimate(
            flops=4 * count * rows * total * (latent_width + LATENT),
            bytes_accessed=count * (rows * 320 + 2 * NOPE * LATENT) * 2 + 4 * total * latent_width,
            transcendentals=count * rows * total,
        ),
    )(query_start, queries_t, key_absorb, value_absorb, keys, keys_t)


def on_device(
    queries,
    latents,
    key_absorb,
    value_absorb,
    out_proj,
    residual_in,
    norm_gain,
    expert_gate,
    expert_up,
    expert_down,
    route_ids,
    route_weights,
):
    rows = queries.shape[0]
    local_heads = queries.shape[1]
    columns = out_proj.shape[1]
    ctx_count = lax.axis_size("ctx")
    ep_count = lax.axis_size("ep")
    ep_me = lax.axis_index("ep")
    owned = rows // ep_count
    query_start = (lax.axis_index("ctx") * rows).astype(jnp.int32).reshape(1)

    keys = lax.all_gather(latents, "ctx", axis=0, tiled=True)
    keys_t = keys.T
    queries_t = jnp.transpose(queries, (1, 2, 0))

    count = local_heads // CHUNKS
    depth = count * VHEAD
    complete = jnp.zeros((ctx_count * owned, columns), jnp.float32)
    before = None
    for chunk in range(CHUNKS):
        heads = attention(
            chunk, count, query_start, queries_t, key_absorb, value_absorb, keys, keys_t
        )
        pieces = [lax.dynamic_slice_in_dim(heads, ep_me * owned, owned, axis=0)]
        for shift in range(1, ep_count):
            target = lax.rem(ep_me + shift, ep_count)
            block = lax.dynamic_slice_in_dim(heads, target * owned, owned, axis=0)
            pieces.append(
                lax.ppermute(
                    block, "ep", [(i, (i + shift) % ep_count) for i in range(ep_count)]
                )
            )
        mine = jnp.concatenate(pieces, axis=1)
        if before is not None:
            mine, before = lax.optimization_barrier((mine, before))
        gathered = lax.all_gather(mine, "ctx", axis=0, tiled=True)
        before = gathered[:8, :128]
        for shift in range(ep_count):
            source = lax.rem(ep_me - shift + ep_count, ep_count)
            weight = lax.dynamic_slice_in_dim(
                out_proj, source * (local_heads * VHEAD) + chunk * depth, depth, axis=0
            )
            complete = complete + jnp.dot(
                gathered[:, shift * depth : (shift + 1) * depth],
                weight,
                preferred_element_type=jnp.float32,
            )
    complete = complete.astype(jnp.bfloat16).reshape(ctx_count, -1, columns)
    attended = lax.all_to_all(complete, "ctx", split_axis=0, concat_axis=2, tiled=True).reshape(
        -1, columns * ctx_count
    )
    wide = residual_in.astype(jnp.float32) + attended.astype(jnp.float32)
    hidden = wide.astype(jnp.bfloat16)
    hidden_wide = hidden.astype(jnp.float32)
    square = jnp.mean(hidden_wide * hidden_wide, axis=1, keepdims=True)
    normed = (hidden_wide * lax.rsqrt(square + 1e-06) * norm_gain).astype(jnp.bfloat16)
    tokens_here = hidden.shape[0]
    window = ep_count
    flat_ids = route_ids.reshape(-1)
    chosen = (flat_ids[:, None] == jnp.arange(window, dtype=jnp.int32)[None, :]).astype(jnp.int32)
    earlier = jnp.cumsum(chosen, axis=0) - chosen
    slot = jnp.sum(earlier * chosen, axis=1)
    place = chosen[:, :, None] * (
        slot[:, None, None] == jnp.arange(CAP, dtype=jnp.int32)[None, None, :]
    ).astype(jnp.int32)
    place = place.reshape(tokens_here, TOPK, window * CAP).astype(jnp.float32)
    gather_table = jnp.sum(place, axis=1).astype(jnp.bfloat16)
    combine_table = jnp.sum(place * route_weights[:, :, None], axis=1)
    outgoing = lax.dot_general(
        gather_table, normed, (((0,), (0,)), ((), ())), preferred_element_type=jnp.float32
    ).astype(jnp.bfloat16)
    outgoing = outgoing.reshape(window, CAP, -1)
    arrived = lax.all_to_all(outgoing, "ep", split_axis=0, concat_axis=0, tiled=True)
    gate_weight = expert_gate[0]
    up_weight = expert_up[0]
    down_weight = expert_down[0]

    flat_rows = lax.all_gather(arrived, "ctx", axis=0, tiled=True).reshape(
        ctx_count * window * CAP, -1
    )
    gate = jnp.dot(flat_rows, gate_weight, preferred_element_type=jnp.float32)
    upper = jnp.dot(flat_rows, up_weight, preferred_element_type=jnp.float32)
    activated = (jax.nn.silu(gate) * upper).astype(jnp.bfloat16)
    partial_out = jnp.dot(activated, down_weight, preferred_element_type=jnp.float32)
    partial_out = partial_out.astype(jnp.bfloat16).reshape(ctx_count, window * CAP, -1)
    parts = lax.all_to_all(partial_out, "ctx", split_axis=0, concat_axis=0, tiled=True)
    result = jnp.sum(parts.astype(jnp.float32), axis=0).astype(jnp.bfloat16)
    result = result.reshape(window, CAP, -1)
    returned = lax.all_to_all(result, "ep", split_axis=0, concat_axis=0, tiled=True)
    mixture = jnp.dot(
        combine_table,
        returned.reshape(window * CAP, -1).astype(jnp.float32),
        precision=lax.Precision.HIGHEST,
    )
    return (hidden_wide + mixture).astype(jnp.bfloat16)


def solution(mesh):
    placed = (
        P("ctx", "ep", None),
        P("ctx", None),
        P("ep", None, None),
        P("ep", None, None),
        P(None, "ctx"),
        P(("ctx", "ep"), None),
        P(),
        P("ep", None, "ctx"),
        P("ep", None, "ctx"),
        P("ep", "ctx", None),
        P(("ctx", "ep"), None),
        P(("ctx", "ep"), None),
    )
    return jax.shard_map(
        on_device, mesh=mesh, in_specs=placed, out_specs=P(("ctx", "ep"), None), check_vma=False
    )
```

time: 505 us -> 367 us (0.73)
  Pallas kernels: 0 us -> 102 us
  waiting for transfers between devices: 178 us -> 80.2 us
  matrix products: 176 us -> 81 us
  blocking collectives: 83.3 us -> 43.9 us
  other arithmetic: 34.3 us -> 5.93 us
  starting transfers between devices: 3.77 us -> 26.5 us
    pallas_call x0 -> x4, Pallas kernels: none -> 102 us  [attention(): pl.pallas_call(attention_kernel, grid_spec=pltpu.PrefetchScalarGridSpec(n...]
    dot_general x14 -> x18, matrix products: 174 us -> 78.7 us  [the longest x16 70.5 us: on_device(): jnp.dot(gathered[:, shift * depth:(shift + 1) * depth], weight, preferred...]
    all_gather x2 -> x5, waiting for transfers between devices: 111 us -> 34 us  [the longest x1 34 us: on_device(): keys = lax.all_gather(latents, 'ctx', axis=0, tiled=True)]
    unnamed x4 -> x5, waiting for transfers between devices: 53.8 us -> 0.78 us
    all_to_all x1, blocking collectives: 53.2 us -> 16.5 us  [on_device(): lax.all_to_all(partial_out, 'ctx', split_axis=0, concat_axis=0, tiled=True)]
    ppermute x0 -> x12, waiting for transfers between devices: none -> 32.1 us  [on_device(): lax.ppermute(block, 'ep', [(i, (i + shift) % ep_count) for i in range(ep_...]
    reduce_sum x2 -> x1, other arithmetic: 26.3 us -> 0.13 us  [on_device(): result = jnp.sum(parts.astype(jnp.float32), axis=0).astype(jnp.bfloat16)]
    ppermute x0 -> x12, starting transfers between devices: none -> 22.6 us  [on_device(): lax.ppermute(block, 'ep', [(i, (i + shift) % ep_count) for i in range(ep_...]
  transfers between devices with their start and end apart: 4 -> 18, of which waited for: 4 -> 11; matrix products, arithmetic and copies ran while one was open for 2% -> 15% of each run, Pallas kernels for 0% -> 21%
where the time goes in v1:
time: 367 us; the launch traced here: 366 us
  Pallas kernels  102 us (28%)
  matrix products  81 us (22%)
  waiting for transfers between devices  80.2 us (22%)
  blocking collectives  43.9 us (12%)
  starting transfers between devices  26.5 us (7%)
  between operations  13.6 us (4%)
  local copies, waits for them, and re-layouts  12.7 us (3%)
  other arithmetic  5.93 us (2%)
    pallas_call x4, Pallas kernels, attention(): pl.pallas_call(attention_kernel, grid_spec=pltpu.PrefetchScalarGridSpec(n...  102 us
    dot_general x16, matrix products, on_device(): jnp.dot(gathered[:, shift * depth:(shift + 1) * depth], weight, preferred...  70.5 us
    all_gather x1, waiting for transfers between devices, on_device(): keys = lax.all_gather(latents, 'ctx', axis=0, tiled=True)  34 us
    ppermute x12, waiting for transfers between devices, on_device(): lax.ppermute(block, 'ep', [(i, (i + shift) % ep_count) for i in range(ep_...  32.1 us
    ppermute x12, starting transfers between devices, on_device(): lax.ppermute(block, 'ep', [(i, (i + shift) % ep_count) for i in range(ep_...  22.6 us
    all_to_all x1, blocking collectives, on_device(): lax.all_to_all(partial_out, 'ctx', split_axis=0, concat_axis=0, tiled=True)  16.5 us
    all_to_all x1, waiting for transfers between devices, on_device(): lax.all_to_all(complete, 'ctx', split_axis=0, concat_axis=2, tiled=True)  13.4 us
    all_gather x1, blocking collectives, on_device(): lax.all_gather(arrived, 'ctx', axis=0, tiled=True)  9.7 us
  transfers between devices with their start and end apart: 18, of which 11 were waited for; matrix products, arithmetic and copies ran while one was open for 15% of the time, Pallas kernels for 21%

profile of v1, /device:TPU:0, one launch (start us, length us, event | category | flops | bytes accessed | tf_op | source)
XLA Modules:
  0.0 365.6 jit_solution(10917855680605783854)
XLA Ops:
  6.5 0.7 all-gather.6.cloned.1.call-update
  7.3 34.0 %all-gather.6.cloned.1.call-done = bf16[2048,576]{0,1:T(8,128)(2,1)} async-done(((bf16[256,576]{0,1:T(8,128)(2,1)}), bf16[2048,576]{0,1:T(8,128)(2,1)}) %all-gather.6.cloned.1.call-update) | async-done | bytes 2359312 | tf_op jit(solution)/shard_map/all_gather | solution.py:118
  41.3 3.1 copy.28.lat_ref
  44.4 1.7 copy-done
  46.1 25.4 %shard_map.119 = bf16[256,1024]{1,0:T(8,128)(2,1)S(1)} custom-call(s32[1]{0:T(128)} %bitcast.start_ref, bf16[32,192,256]{2,1,0:T(8,128)(2,1)} %bitcast.67, bf16[32,128,512]{2,1,0:T(8,128)(2,1)} %ka_ref.7, bf16[32,512,128]{2,1,0:T(8,128)(2,1)} %va_ref.7, bf16[2048,576]{1,0:T(8,128)(2,1)S(1)} %copy.28.lat_ref, bf16[576,2048]{1,0:T(8,128)(2,1)S(1)} %bitcast.61), custom_call_target="tpu_custom_call" | custom-call | flops 18253611008 | bytes 8126464 | tf_op jit(solution)/shard_map/pallas_call | solution.py:67
  71.6 1.5 collective-permute-start.3
  73.1 2.4 collective-permute-start.4
  75.5 1.4 collective-permute-start.5
  77.0 2.9 collective-permute-done.3
  79.9 4.9 %collective-permute-done.4 = bf16[64,1024]{1,0:T(8,128)(2,1)S(1)} collective-permute-done((bf16[64,1024]{1,0:T(8,128)(2,1)S(1)}, bf16[64,1024]{1,0:T(8,128)(2,1)S(1)}, u32[]{:S(2)}, u32[]{:S(2)}) %collective-permute-start.4) | collective-permute-done | bytes 131104 | tf_op jit(solution)/shard_map/ppermute | solution.py:135
  84.8 0.9 pad_maximum_fusion.1
  85.8 1.7 copy-done.1
  87.5 25.4 %shard_map.118 = bf16[256,1024]{1,0:T(8,128)(2,1)S(1)} custom-call(s32[1]{0:T(128)} %bitcast.start_ref, bf16[32,192,256]{2,1,0:T(8,128)(2,1)} %bitcast.68, bf16[32,128,512]{2,1,0:T(8,128)(2,1)} %ka_ref.7, bf16[32,512,128]{2,1,0:T(8,128)(2,1)} %va_ref.7, bf16[2048,576]{1,0:T(8,128)(2,1)S(1)} %copy.28.lat_ref, bf16[576,2048]{1,0:T(8,128)(2,1)S(1)} %bitcast.62), custom_call_target="tpu_custom_call" | custom-call | flops 18253611008 | bytes 8126464 | tf_op jit(solution)/shard_map/pallas_call | solution.py:67
  112.9 3.3 collective-permute-start
  116.3 1.5 collective-permute-start.1
  117.8 0.9 collective-permute-start.2
  118.7 2.8 collective-permute-done
  121.5 4.5 %collective-permute-done.1 = bf16[64,1024]{1,0:T(8,128)(2,1)S(1)} collective-permute-done((bf16[64,1024]{1,0:T(8,128)(2,1)S(1)}, bf16[64,1024]{1,0:T(8,128)(2,1)S(1)}, u32[]{:S(2)}, u32[]{:S(2)}) %collective-permute-start.1) | collective-permute-done | bytes 131104 | tf_op jit(solution)/shard_map/ppermute | solution.py:135
  126.0 0.8 pad_maximum_fusion
  127.0 1.7 copy-done.2
  128.6 25.4 %shard_map.120 = bf16[256,1024]{1,0:T(8,128)(2,1)S(1)} custom-call(s32[1]{0:T(128)} %bitcast.start_ref, bf16[32,192,256]{2,1,0:T(8,128)(2,1)} %bitcast.69, bf16[32,128,512]{2,1,0:T(8,128)(2,1)} %ka_ref.7, bf16[32,512,128]{2,1,0:T(8,128)(2,1)} %va_ref.7, bf16[2048,576]{1,0:T(8,128)(2,1)S(1)} %copy.28.lat_ref, bf16[576,2048]{1,0:T(8,128)(2,1)S(1)} %bitcast.63), custom_call_target="tpu_custom_call" | custom-call | flops 18253611008 | bytes 8126464 | tf_op jit(solution)/shard_map/pallas_call | solution.py:67
  154.1 3.3 collective-permute-start.6
  157.5 2.0 collective-permute-start.7
  159.5 0.4 collective-permute-start.8
  159.9 3.5 collective-permute-done.6
  163.4 4.4 %collective-permute-done.7 = bf16[64,1024]{1,0:T(8,128)(2,1)S(1)} collective-permute-done((bf16[64,1024]{1,0:T(8,128)(2,1)S(1)}, bf16[64,1024]{1,0:T(8,128)(2,1)S(1)}, u32[]{:S(2)}, u32[]{:S(2)}) %collective-permute-start.7) | collective-permute-done | bytes 131104 | tf_op jit(solution)/shard_map/ppermute | solution.py:135
  167.8 0.8 pad_maximum_fusion.2
  168.7 1.7 copy-done.3
  170.3 25.4 %shard_map.121 = bf16[256,1024]{1,0:T(8,128)(2,1)S(1)} custom-call(s32[1]{0:T(128)} %bitcast.start_ref, bf16[32,192,256]{2,1,0:T(8,128)(2,1)} %bitcast.70, bf16[32,128,512]{2,1,0:T(8,128)(2,1)} %ka_ref.7, bf16[32,512,128]{2,1,0:T(8,128)(2,1)} %va_ref.7, bf16[2048,576]{1,0:T(8,128)(2,1)S(1)} %copy.28.lat_ref, bf16[576,2048]{1,0:T(8,128)(2,1)S(1)} %bitcast.64), custom_call_target="tpu_custom_call" | custom-call | flops 18253611008 | bytes 8126464 | tf_op jit(solution)/shard_map/pallas_call | solution.py:67
  195.8 2.3 collective-permute-start.10
  198.2 3.4 collective-permute-start.11
  201.5 2.8 collective-permute-done.10
  204.3 1.1 collective-permute-done.11
  205.5 5.1 %collective-permute-done.9 = bf16[64,1024]{1,0:T(8,128)(2,1)S(1)} collective-permute-done((bf16[64,1024]{1,0:T(8,128)(2,1)S(1)}, bf16[64,1024]{1,0:T(8,128)(2,1)S(1)}, u32[]{:S(2)}, u32[]{:S(2)}) %collective-permute-start.9) | collective-permute-done | bytes 131104 | tf_op jit(solution)/shard_map/ppermute | solution.py:135
  210.6 0.8 pad_maximum_fusion.3
  211.8 1.4 reduce-window.6
  213.7 3.2 fusion.26
  216.9 4.2 %fusion.28 = f32[512,896]{1,0:T(8,128)} fusion(bf16[16384,896]{1,0:T(8,128)(2,1)} %param.16, s32[]{:T(128)S(6)} %select_n.82, bf16[512,4096]{1,0:T(8,128)(2,1)S(1)} %copy-done.16), kind=kOutput, calls=%fused_computation.36 | convolution fusion | flops 939524096 | bytes 4718596 | tf_op jit(solution)/shard_map/dot_general | solution.py:149
  221.1 4.0 %fusion.30 = f32[512,896]{1,0:T(8,128)} fusion(bf16[16384,896]{1,0:T(8,128)(2,1)} %param.16, s32[]{:T(128)S(6)} %select_n.81, bf16[512,4096]{1,0:T(8,128)(2,1)S(1)} %copy-done.16), kind=kOutput, calls=%fused_computation.38 | convolution fusion | flops 939524096 | bytes 4718596 | tf_op jit(solution)/shard_map/dot_general | solution.py:149
  225.1 4.1 %fusion.32 = f32[512,896]{1,0:T(8,128)} fusion(bf16[16384,896]{1,0:T(8,128)(2,1)} %param.16, s32[]{:T(128)S(6)} %select_n.80, bf16[512,4096]{1,0:T(8,128)(2,1)S(1)} %copy-done.16), kind=kOutput, calls=%fused_computation.40 | convolution fusion | flops 939524096 | bytes 4718596 | tf_op jit(solution)/shard_map/dot_general | solution.py:149
  229.2 4.4 %fusion.34 = f32[512,896]{1,0:T(8,128)} fusion(bf16[16384,896]{1,0:T(8,128)(2,1)} %param.16, s32[]{:T(128)S(6)} %select_n.79, bf16[512,4096]{1,0:T(8,128)(2,1)} %all-gather.8.cloned.1.call-done), kind=kOutput, calls=%fused_computation.42 | convolution fusion | flops 939524096 | bytes 4718596 | tf_op jit(solution)/shard_map/dot_general | solution.py:149
  233.6 4.0 %fusion.36 = f32[512,896]{1,0:T(8,128)} fusion(bf16[16384,896]{1,0:T(8,128)(2,1)} %param.16, s32[]{:T(128)S(6)} %select_n.78, bf16[512,4096]{1,0:T(8,128)(2,1)S(1)} %copy-done.17), kind=kOutput, calls=%fused_computation.44 | convolution fusion | flops 939524096 | bytes 4718596 | tf_op jit(solution)/shard_map/dot_general | solution.py:149
  237.6 4.1 %fusion.38 = f32[512,896]{1,0:T(8,128)} fusion(bf16[16384,896]{1,0:T(8,128)(2,1)} %param.16, s32[]{:T(128)S(6)} %select_n.77, bf16[512,4096]{1,0:T(8,128)(2,1)S(1)} %copy-done.17), kind=kOutput, calls=%fused_computation.46 | convolution fusion | flops 939524096 | bytes 4718596 | tf_op jit(solution)/shard_map/dot_general | solution.py:149
  241.7 4.1 %fusion.40 = f32[512,896]{1,0:T(8,128)} fusion(bf16[16384,896]{1,0:T(8,128)(2,1)} %param.16, s32[]{:T(128)S(6)} %select_n.76, bf16[512,4096]{1,0:T(8,128)(2,1)S(1)} %copy-done.17), kind=kOutput, calls=%fused_computation.48 | convolution fusion | flops 939524096 | bytes 4718596 | tf_op jit(solution)/shard_map/dot_general | solution.py:149
  245.8 4.5 %fusion.20 = f32[512,896]{1,0:T(8,128)} fusion(bf16[16384,896]{1,0:T(8,128)(2,1)} %param.16, s32[]{:T(128)S(6)} %select_n.86, bf16[512,4096]{1,0:T(8,128)(2,1)} %all-gather.12.cloned.1.call-done), kind=kOutput, calls=%fused_computation.28 | convolution fusion | flops 939524096 | bytes 4718596 | tf_op jit(solution)/shard_map/dot_general | solution.py:149
  250.3 4.0 %fusion.22 = f32[512,896]{1,0:T(8,128)} fusion(bf16[16384,896]{1,0:T(8,128)(2,1)} %param.16, s32[]{:T(128)S(6)} %select_n.85, bf16[512,4096]{1,0:T(8,128)(2,1)S(1)} %copy-done.18), kind=kOutput, calls=%fused_computation.30 | convolution fusion | flops 939524096 | bytes 4718596 | tf_op jit(solution)/shard_map/dot_general | solution.py:149
  254.3 4.0 %fusion.24 = f32[512,896]{1,0:T(8,128)} fusion(bf16[16384,896]{1,0:T(8,128)(2,1)} %param.16, s32[]{:T(128)S(6)} %select_n.84, bf16[512,4096]{1,0:T(8,128)(2,1)S(1)} %copy-done.18), kind=kOutput, calls=%fused_computation.32 | convolution fusion | flops 939524096 | bytes 4718596 | tf_op jit(solution)/shard_map/dot_general | solution.py:149
  258.3 4.1 %fusion.18 = f32[512,896]{1,0:T(8,128)} fusion(bf16[16384,896]{1,0:T(8,128)(2,1)} %param.16, s32[]{:T(128)S(6)} %select_n.87, bf16[512,4096]{1,0:T(8,128)(2,1)S(1)} %copy-done.18), kind=kOutput, calls=%fused_computation.26 | convolution fusion | flops 939524096 | bytes 4718596 | tf_op jit(solution)/shard_map/dot_general | solution.py:149
  262.4 4.4 %fusion.14 = f32[512,896]{1,0:T(8,128)} fusion(bf16[16384,896]{1,0:T(8,128)(2,1)} %param.16, s32[]{:T(128)S(6)} %select_n.89, bf16[512,4096]{1,0:T(8,128)(2,1)} %all-gather.14.cloned.1.call-done), kind=kOutput, calls=%fused_computation.22 | convolution fusion | flops 939524096 | bytes 4718596 | tf_op jit(solution)/shard_map/dot_general | solution.py:149
  266.9 4.5 %fusion.16 = f32[512,896]{1,0:T(8,128)} fusion(bf16[16384,896]{1,0:T(8,128)(2,1)} %param.16, s32[]{:T(128)S(6)} %select_n.88, bf16[512,4096]{1,0:T(8,128)(2,1)} %all-gather.14.cloned.1.call-done), kind=kOutput, calls=%fused_computation.24 | convolution fusion | flops 939524096 | bytes 4718596 | tf_op jit(solution)/shard_map/dot_general | solution.py:149
  271.3 4.6 %fusion.12 = f32[512,896]{1,0:T(8,128)} fusion(bf16[16384,896]{1,0:T(8,128)(2,1)} %param.16, s32[]{:T(128)S(6)} %select_n.90, bf16[512,4096]{1,0:T(8,128)(2,1)} %all-gather.14.cloned.1.call-done), kind=kOutput, calls=%fused_computation.20 | convolution fusion | flops 939524096 | bytes 4718596 | tf_op jit(solution)/shard_map/dot_general | solution.py:149
  276.0 8.3 %add_convert_fusion.1 = bf16[512,896]{1,0:T(8,128)(2,1)} fusion(f32[512,896]{1,0:T(8,128)} %fusion.12, f32[512,896]{1,0:T(8,128)} %fusion.14, f32[512,896]{1,0:T(8,128)} %fusion.16, f32[512,896]{1,0:T(8,128)} %fusion.18, f32[512,896]{1,0:T(8,128)S(1)} %copy-done.11, f32[512,896]{1,0:T(8,128)S(1)} %copy-done.12, f32[512,896]{1,0:T(8,128)} %fusion.24, ...), kind=kOutput, calls=%fused_computation.17 | convolution fusion | flops 946864128 | bytes 31326212 | tf_op jit(solution)/shard_map/dot_general | solution.py:149
  284.3 3.7 %all-to-all-start = ((bf16[8,64,896]{2,1,0:T(8,128)(2,1)}), bf16[8,64,896]{2,1,0:T(8,128)(2,1)S(1)}, u32[]{:S(2)}, u32[]{:S(2)}) async-start(bf16[8,64,896]{2,1,0:T(8,128)(2,1)} %bitcast.3), calls=%async_computation | async-start | bytes 1835008 | tf_op jit(solution)/shard_map/all_to_all | solution.py:155
  288.5 13.4 %all-to-all-done = bf16[8,64,896]{2,1,0:T(8,128)(2,1)S(1)} async-done(((bf16[8,64,896]{2,1,0:T(8,128)(2,1)}), bf16[8,64,896]{2,1,0:T(8,128)(2,1)S(1)}, u32[]{:S(2)}, u32[]{:S(2)}) %all-to-all-start) | async-done | bytes 917536 | tf_op jit(solution)/shard_map/all_to_all | solution.py:155
  302.2 1.0 copy-done.13
  303.3 0.4 fusion.7
  304.0 0.4 convolution_convert_fusion.1
  304.5 9.3 %all_to_all.24 = bf16[4,2,7168]{2,1,0:T(2,128)(2,1)S(1)} all-to-all(bf16[4,2,7168]{2,1,0:T(2,128)(2,1)S(1)} %reshape.109), channel_id=1, replica_groups=mesh['ctx'=8,'ep'=4] {'ep'}, dimensions={0} | all-to-all | bytes 229376 | tf_op jit(solution)/shard_map/all_to_all | solution.py:179
  313.7 9.7 %all_gather.23 = bf16[32,2,7168]{2,1,0:T(2,128)(2,1)S(1)} all-gather(bf16[4,2,7168]{2,1,0:T(2,128)(2,1)S(1)} %all_to_all.24), channel_id=1, replica_groups=mesh['ctx'=8,'ep'=4] {'ctx'}, dimensions={0}, use_global_device_ids=true | all-gather | bytes 1032192 | tf_op jit(solution)/shard_map/all_gather | solution.py:184
  323.8 2.8 fusion.5
  326.5 5.5 %fusion.1 = bf16[8,8,7168]{2,1,0:T(8,128)(2,1)S(1)} fusion(bf16[1,256,7168]{2,1,0:T(8,128)(2,1)} %param.21, bf16[64,7168]{1,0:T(8,128)(2,1)S(1)} %reshape.110, bf16[1,7168,256]{2,1,0:T(8,128)(2,1)} %param.20, f32[64,256]{1,0:T(8,128)S(1)} %fusion.5), kind=kOutput, calls=%fused_computation.3 | convolution fusion | flops 470319104 | bytes 9240576 | tf_op jit(solution)/shard_map/dot_general | solution.py:190
  332.0 16.5 %all_to_all.25 = bf16[8,8,7168]{2,1,0:T(8,128)(2,1)S(1)} all-to-all(bf16[8,8,7168]{2,1,0:T(8,128)(2,1)S(1)} %fusion.1), channel_id=1, replica_groups=mesh['ctx'=8,'ep'=4] {'ctx'}, dimensions={0} | all-to-all | bytes 1835008 | tf_op jit(solution)/shard_map/all_to_all | solution.py:192
  348.7 8.4 %all_to_all.26 = bf16[4,2,7168]{2,1,0:T(2,128)(2,1)S(1)} all-to-all(bf16[4,2,7168]{2,1,0:T(2,128)(2,1)S(1)} %reshape.112), channel_id=1, replica_groups=mesh['ctx'=8,'ep'=4] {'ep'}, dimensions={0} | all-to-all | bytes 229376 | tf_op jit(solution)/shard_map/all_to_all | solution.py:195
  357.2 1.9 fusion
  (78 shorter events, 3.0 us)
Async XLA Ops:
  6.5 34.8 %all-gather.6.cloned.1.call-start = ((), (), s32[]{:S(2)}) async-start(), calls=%async_computation.4 | async-start | bytes 2654208 | tf_op jit(solution)/shard_map/all_gather | solution.py:118
  7.3 206.4 %all-gather.10.cloned.1.call-start = ((), (), s32[]{:S(2)}) async-start(), calls=%async_computation.6 | async-start | bytes 4718592 | tf_op jit(solution)/shard_map/all_gather | solution.py:142
  44.4 1.7 copy-start
  71.6 8.3 %collective-permute-start.3 = (bf16[64,1024]{1,0:T(8,128)(2,1)S(1)}, bf16[64,1024]{1,0:T(8,128)(2,1)S(1)}, u32[]{:S(2)}, u32[]{:S(2)}) collective-permute-start(bf16[64,1024]{1,0:T(8,128)(2,1)S(1)} %get-tuple-element.16), channel_id=1, source_target_pairs={{0,1},{1,2},{2,3},{3,0},{4,5},{5,6},{6,7},{7,4},{8,9},{9,10},{10,1... | collective-permute-start | bytes 393224 | tf_op jit(solution)/shard_map/ppermute | solution.py:135
  73.1 11.7 %collective-permute-start.4 = (bf16[64,1024]{1,0:T(8,128)(2,1)S(1)}, bf16[64,1024]{1,0:T(8,128)(2,1)S(1)}, u32[]{:S(2)}, u32[]{:S(2)}) collective-permute-start(bf16[64,1024]{1,0:T(8,128)(2,1)S(1)} %get-tuple-element.15), channel_id=1, source_target_pairs={{0,2},{1,3},{2,0},{3,1},{4,6},{5,7},{6,4},{7,5},{8,10},{9,11},{10,... | collective-permute-start | bytes 393224 | tf_op jit(solution)/shard_map/ppermute | solution.py:135
  75.5 9.3 %collective-permute-start.5 = (bf16[64,1024]{1,0:T(8,128)(2,1)S(1)}, bf16[64,1024]{1,0:T(8,128)(2,1)S(1)}, u32[]{:S(2)}, u32[]{:S(2)}) collective-permute-start(bf16[64,1024]{1,0:T(8,128)(2,1)S(1)} %get-tuple-element.14), channel_id=1, source_target_pairs={{0,3},{1,0},{2,1},{3,2},{4,7},{5,4},{6,5},{7,6},{8,11},{9,8},{10,9... | collective-permute-start | bytes 393224 | tf_op jit(solution)/shard_map/ppermute | solution.py:135
  85.7 143.4 %all-gather.8.cloned.1.call-start = ((), (), s32[]{:S(2)}) async-start(), calls=%async_computation.5 | async-start | bytes 4718592 | tf_op jit(solution)/shard_map/all_gather | solution.py:142
  85.8 1.7 copy-start.1
  112.9 8.6 %collective-permute-start = (bf16[64,1024]{1,0:T(8,128)(2,1)S(1)}, bf16[64,1024]{1,0:T(8,128)(2,1)S(1)}, u32[]{:S(2)}, u32[]{:S(2)}) collective-permute-start(bf16[64,1024]{1,0:T(8,128)(2,1)S(1)} %get-tuple-element.12), channel_id=1, source_target_pairs={{0,1},{1,2},{2,3},{3,0},{4,5},{5,6},{6,7},{7,4},{8,9},{9,10},{10,1... | collective-permute-start | bytes 393224 | tf_op jit(solution)/shard_map/ppermute | solution.py:135
  116.3 9.8 %collective-permute-start.1 = (bf16[64,1024]{1,0:T(8,128)(2,1)S(1)}, bf16[64,1024]{1,0:T(8,128)(2,1)S(1)}, u32[]{:S(2)}, u32[]{:S(2)}) collective-permute-start(bf16[64,1024]{1,0:T(8,128)(2,1)S(1)} %get-tuple-element.11), channel_id=1, source_target_pairs={{0,2},{1,3},{2,0},{3,1},{4,6},{5,7},{6,4},{7,5},{8,10},{9,11},{10,... | collective-permute-start | bytes 393224 | tf_op jit(solution)/shard_map/ppermute | solution.py:135
  117.8 8.3 %collective-permute-start.2 = (bf16[64,1024]{1,0:T(8,128)(2,1)S(1)}, bf16[64,1024]{1,0:T(8,128)(2,1)S(1)}, u32[]{:S(2)}, u32[]{:S(2)}) collective-permute-start(bf16[64,1024]{1,0:T(8,128)(2,1)S(1)} %get-tuple-element.10), channel_id=1, source_target_pairs={{0,3},{1,0},{2,1},{3,2},{4,7},{5,4},{6,5},{7,6},{8,11},{9,8},{10,9... | collective-permute-start | bytes 393224 | tf_op jit(solution)/shard_map/ppermute | solution.py:135
  126.9 118.9 %all-gather.12.cloned.1.call-start = ((), (), s32[]{:S(2)}) async-start(), calls=%async_computation.7 | async-start | bytes 4718592 | tf_op jit(solution)/shard_map/all_gather | solution.py:142
  127.0 1.7 copy-start.2
  154.1 9.2 %collective-permute-start.6 = (bf16[64,1024]{1,0:T(8,128)(2,1)S(1)}, bf16[64,1024]{1,0:T(8,128)(2,1)S(1)}, u32[]{:S(2)}, u32[]{:S(2)}) collective-permute-start(bf16[64,1024]{1,0:T(8,128)(2,1)S(1)} %get-tuple-element.20), channel_id=1, source_target_pairs={{0,1},{1,2},{2,3},{3,0},{4,5},{5,6},{6,7},{7,4},{8,9},{9,10},{10,1... | collective-permute-start | bytes 393224 | tf_op jit(solution)/shard_map/ppermute | solution.py:135
  157.5 10.3 %collective-permute-start.7 = (bf16[64,1024]{1,0:T(8,128)(2,1)S(1)}, bf16[64,1024]{1,0:T(8,128)(2,1)S(1)}, u32[]{:S(2)}, u32[]{:S(2)}) collective-permute-start(bf16[64,1024]{1,0:T(8,128)(2,1)S(1)} %get-tuple-element.19), channel_id=1, source_target_pairs={{0,2},{1,3},{2,0},{3,1},{4,6},{5,7},{6,4},{7,5},{8,10},{9,11},{10,... | collective-permute-start | bytes 393224 | tf_op jit(solution)/shard_map/ppermute | solution.py:135
  159.5 8.3 %collective-permute-start.8 = (bf16[64,1024]{1,0:T(8,128)(2,1)S(1)}, bf16[64,1024]{1,0:T(8,128)(2,1)S(1)}, u32[]{:S(2)}, u32[]{:S(2)}) collective-permute-start(bf16[64,1024]{1,0:T(8,128)(2,1)S(1)} %get-tuple-element.18), channel_id=1, source_target_pairs={{0,3},{1,0},{2,1},{3,2},{4,7},{5,4},{6,5},{7,6},{8,11},{9,8},{10,9... | collective-permute-start | bytes 393224 | tf_op jit(solution)/shard_map/ppermute | solution.py:135
  168.6 93.8 %all-gather.14.cloned.1.call-start = ((), (), s32[]{:S(2)}) async-start(), calls=%async_computation.8 | async-start | bytes 4718592 | tf_op jit(solution)/shard_map/all_gather | solution.py:142
  168.7 1.7 copy-start.3
  195.8 15.7 %copy-start.14 = (s32[64,8]{0,1:T(8,128)S(1)}, s32[64,8]{0,1:T(8,128)}, u32[]{:S(2)}) copy-start(s32[64,8]{0,1:T(8,128)} %param.22) | copy-start | bytes 6148
  195.8 8.5 %collective-permute-start.10 = (bf16[64,1024]{1,0:T(8,128)(2,1)S(1)}, bf16[64,1024]{1,0:T(8,128)(2,1)S(1)}, u32[]{:S(2)}, u32[]{:S(2)}) collective-permute-start(bf16[64,1024]{1,0:T(8,128)(2,1)S(1)} %get-tuple-element.23), channel_id=1, source_target_pairs={{0,2},{1,3},{2,0},{3,1},{4,6},{5,7},{6,4},{7,5},{8,10},{9,11},{10,... | collective-permute-start | bytes 393224 | tf_op jit(solution)/shard_map/ppermute | solution.py:135
  198.2 7.3 %collective-permute-start.11 = (bf16[64,1024]{1,0:T(8,128)(2,1)S(1)}, bf16[64,1024]{1,0:T(8,128)(2,1)S(1)}, u32[]{:S(2)}, u32[]{:S(2)}) collective-permute-start(bf16[64,1024]{1,0:T(8,128)(2,1)S(1)} %get-tuple-element.22), channel_id=1, source_target_pairs={{0,3},{1,0},{2,1},{3,2},{4,7},{5,4},{6,5},{7,6},{8,11},{9,8},{10,9... | collective-permute-start | bytes 393224 | tf_op jit(solution)/shard_map/ppermute | solution.py:135
  201.5 9.1 %collective-permute-start.9 = (bf16[64,1024]{1,0:T(8,128)(2,1)S(1)}, bf16[64,1024]{1,0:T(8,128)(2,1)S(1)}, u32[]{:S(2)}, u32[]{:S(2)}) collective-permute-start(bf16[64,1024]{1,0:T(8,128)(2,1)S(1)} %get-tuple-element.24), channel_id=1, source_target_pairs={{0,1},{1,2},{2,3},{3,0},{4,5},{5,6},{6,7},{7,4},{8,9},{9,10},{10,1... | collective-permute-start | bytes 393224 | tf_op jit(solution)/shard_map/ppermute | solution.py:135
  213.7 3.2 copy-start.16
  229.2 4.5 %copy-start.17 = (bf16[512,4096]{1,0:T(8,128)(2,1)S(1)}, bf16[512,4096]{1,0:T(8,128)(2,1)}, u32[]{:S(2)}) copy-start(bf16[512,4096]{1,0:T(8,128)(2,1)} %all-gather.8.cloned.1.call-done) | copy-start | bytes 12582916
  245.8 4.5 %copy-start.18 = (bf16[512,4096]{1,0:T(8,128)(2,1)S(1)}, bf16[512,4096]{1,0:T(8,128)(2,1)}, u32[]{:S(2)}) copy-start(bf16[512,4096]{1,0:T(8,128)(2,1)} %all-gather.12.cloned.1.call-done) | copy-start | bytes 12582916
  262.4 13.5 %copy-start.10 = (f32[512,896]{1,0:T(8,128)S(1)}, f32[512,896]{1,0:T(8,128)}, u32[]{:S(2)}) copy-start(f32[512,896]{1,0:T(8,128)} %fusion.40) | copy-start | bytes 5505028
  262.4 13.5 %copy-start.11 = (f32[512,896]{1,0:T(8,128)S(1)}, f32[512,896]{1,0:T(8,128)}, u32[]{:S(2)}) copy-start(f32[512,896]{1,0:T(8,128)} %fusion.20) | copy-start | bytes 5505028
  262.4 13.5 %copy-start.12 = (f32[512,896]{1,0:T(8,128)S(1)}, f32[512,896]{1,0:T(8,128)}, u32[]{:S(2)}) copy-start(f32[512,896]{1,0:T(8,128)} %fusion.22) | copy-start | bytes 5505028
  266.9 9.0 %copy-start.7 = (f32[512,896]{1,0:T(8,128)S(1)}, f32[512,896]{1,0:T(8,128)}, u32[]{:S(2)}) copy-start(f32[512,896]{1,0:T(8,128)} %fusion.34) | copy-start | bytes 5505028
  266.9 9.1 %copy-start.8 = (f32[512,896]{1,0:T(8,128)S(1)}, f32[512,896]{1,0:T(8,128)}, u32[]{:S(2)}) copy-start(f32[512,896]{1,0:T(8,128)} %fusion.36) | copy-start | bytes 5505028
  266.9 9.1 %copy-start.9 = (f32[512,896]{1,0:T(8,128)S(1)}, f32[512,896]{1,0:T(8,128)}, u32[]{:S(2)}) copy-start(f32[512,896]{1,0:T(8,128)} %fusion.38) | copy-start | bytes 5505028
  271.3 4.6 %copy-start.4 = (f32[512,896]{1,0:T(8,128)S(1)}, f32[512,896]{1,0:T(8,128)}, u32[]{:S(2)}) copy-start(f32[512,896]{1,0:T(8,128)} %fusion.28) | copy-start | bytes 5505028
  271.3 4.6 %copy-start.5 = (f32[512,896]{1,0:T(8,128)S(1)}, f32[512,896]{1,0:T(8,128)}, u32[]{:S(2)}) copy-start(f32[512,896]{1,0:T(8,128)} %fusion.30) | copy-start | bytes 5505028
  271.3 4.6 %copy-start.6 = (f32[512,896]{1,0:T(8,128)S(1)}, f32[512,896]{1,0:T(8,128)}, u32[]{:S(2)}) copy-start(f32[512,896]{1,0:T(8,128)} %fusion.32) | copy-start | bytes 5505028
  284.3 3.9 %copy-start.15 = (f32[64,8]{0,1:T(8,128)S(1)}, f32[64,8]{0,1:T(8,128)}, u32[]{:S(2)}) copy-start(f32[64,8]{0,1:T(8,128)} %param.23) | copy-start | bytes 6148
  284.3 17.6 %all-to-all-start = ((bf16[8,64,896]{2,1,0:T(8,128)(2,1)}), bf16[8,64,896]{2,1,0:T(8,128)(2,1)S(1)}, u32[]{:S(2)}, u32[]{:S(2)}) async-start(bf16[8,64,896]{2,1,0:T(8,128)(2,1)} %bitcast.3), calls=%async_computation | async-start | bytes 1835008 | tf_op jit(solution)/shard_map/all_to_all | solution.py:155
  302.1 1.2 copy-start.13
  303.3 0.7 copy-start.19
Sparse Core Ops, SparseCore 0:
  9.2 32.0 all-gather.5
  85.9 37.6 all-gather.9
  127.0 38.0 all-gather.7
  168.7 37.5 all-gather.11
  211.6 35.7 all-gather.13

commit v2 on v1

--- a/solution.py
+++ b/solution.py
@@ -1,3 +1,5 @@
+import functools
+
 import jax
 import jax.numpy as jnp
 from jax import lax
@@ -12,7 +14,8 @@
 TOPK = 8
 CAP = 2
 CHUNKS = 4
-KEY_BLOCK = 512
+KEY_BLOCK = 256
+GROUP = 4
 LOG2E = 1.4426950408889634
 
 
@@ -20,46 +23,59 @@
     return lax.dot_general(a, b, (((0,), (0,)), ((), ())), preferred_element_type=jnp.float32)
 
 
-def attention_kernel(start_ref, q_ref, ka_ref, va_ref, lat_ref, latt_ref, out_ref, qf_ref, s_ref):
+def attention_kernel(
+    start_ref, q_ref, ka_ref, va_ref, lat_ref, latt_ref, out_ref, qf_ref, even_ref, odd_ref
+):
     factor = (NOPE + ROPE) ** (-0.5) * LOG2E
-    rows = q_ref.shape[2]
+    group, _, rows = q_ref.shape
     keys = lat_ref.shape[0]
     query_start = start_ref[0]
-    absorbed = over_first(ka_ref[0], q_ref[0, :NOPE, :])
-    qf_ref[:LATENT, :] = (absorbed * factor).astype(jnp.bfloat16)
-    qf_ref[LATENT:, :] = (q_ref[0, NOPE:, :].astype(jnp.float32) * factor).astype(jnp.bfloat16)
+    slots = (even_ref, odd_ref)
     ahead = lax.broadcasted_iota(jnp.int32, (KEY_BLOCK, rows), 0) - lax.broadcasted_iota(
         jnp.int32, (KEY_BLOCK, rows), 1
     )
-    top = jnp.full((8, rows), -1e30, jnp.float32)
-    for begin in range(0, keys, KEY_BLOCK):
-        scores = jnp.dot(
-            lat_ref[begin : begin + KEY_BLOCK, :], qf_ref[...], preferred_element_type=jnp.float32
+    for head in range(group):
+        absorbed = over_first(ka_ref[head], q_ref[head, :NOPE, :])
+        qf_ref[head, :LATENT, :] = (absorbed * factor).astype(jnp.bfloat16)
+        qf_ref[head, LATENT:, :] = (q_ref[head, NOPE:, :].astype(jnp.float32) * factor).astype(
+            jnp.bfloat16
         )
-        scores = jnp.where(ahead <= query_start - begin, scores, -1e30)
-        s_ref[begin : begin + KEY_BLOCK, :] = scores
-        top = jnp.maximum(top, jnp.max(scores.reshape(KEY_BLOCK // 8, 8, rows), axis=0))
-    top = jnp.max(top, axis=0, keepdims=True)
-    total = jnp.zeros((8, rows), jnp.float32)
-    mixed = jnp.zeros((LATENT, rows), jnp.float32)
-    for begin in range(0, keys, KEY_BLOCK):
-        weights = jnp.exp2(s_ref[begin : begin + KEY_BLOCK, :] - top)
-        total = total + jnp.sum(weights.reshape(KEY_BLOCK // 8, 8, rows), axis=0)
-        mixed = mixed + jnp.dot(
-            latt_ref[:LATENT, begin : begin + KEY_BLOCK],
-            weights.astype(jnp.bfloat16),
-            preferred_element_type=jnp.float32,
-        )
-    inverse = 1.0 / jnp.sum(total, axis=0, keepdims=True)
-    mixed = (mixed * inverse).astype(jnp.bfloat16)
-    out_ref[...] = over_first(mixed, va_ref[0]).astype(jnp.bfloat16)
+
+    highest = None
+    for step in range(group + 1):
+        top = jnp.full((8, rows), -1e30, jnp.float32)
+        total = jnp.zeros((8, rows), jnp.float32)
+        mixed = jnp.zeros((LATENT, rows), jnp.float32)
+        for begin in range(0, keys, KEY_BLOCK):
+            block = pl.ds(begin, KEY_BLOCK)
+            if step < group:
+                scores = jnp.dot(
+                    lat_ref[block, :], qf_ref[step], preferred_element_type=jnp.float32
+                )
+                scores = jnp.where(ahead <= query_start - begin, scores, -1e30)
+                slots[step % 2][block, :] = scores
+                top = jnp.maximum(top, jnp.max(scores.reshape(KEY_BLOCK // 8, 8, rows), axis=0))
+            if step > 0:
+                weights = jnp.exp2(slots[(step - 1) % 2][block, :] - highest)
+                total = total + jnp.sum(weights.reshape(KEY_BLOCK // 8, 8, rows), axis=0)
+                mixed = mixed + jnp.dot(
+                    latt_ref[:LATENT, block],
+                    weights.astype(jnp.bfloat16),
+                    preferred_element_type=jnp.float32,
+                )
+        if step > 0:
+            inverse = 1.0 / jnp.sum(total, axis=0, keepdims=True)
+            out_ref[:, pl.ds((step - 1) * VHEAD, VHEAD)] = over_first(
+                (mixed * inverse).astype(jnp.bfloat16), va_ref[step - 1]
+            ).astype(jnp.bfloat16)
+        highest = jnp.max(top, axis=0, keepdims=True)
 
 
 def attention(chunk, count, query_start, queries_t, key_absorb, value_absorb, keys, keys_t):
-    rows = queries_t.shape[2]
-    width = queries_t.shape[1]
+    _, width, rows = queries_t.shape
     total, latent_width = keys.shape
-    first = chunk * count
+    group = GROUP if count % GROUP == 0 else 1
+    first = chunk * count // group
 
     def by_head(i, _):
         return (first + i, 0, 0)
@@ -68,28 +84,92 @@
         attention_kernel,
         grid_spec=pltpu.PrefetchScalarGridSpec(
             num_scalar_prefetch=1,
-            grid=(count,),
+            grid=(count // group,),
             in_specs=[
-                pl.BlockSpec((1, width, rows), by_head),
-                pl.BlockSpec((1, NOPE, LATENT), by_head),
-                pl.BlockSpec((1, LATENT, VHEAD), by_head),
+                pl.BlockSpec((group, width, rows), by_head),
+                pl.BlockSpec((group, NOPE, LATENT), by_head),
+                pl.BlockSpec((group, LATENT, VHEAD), by_head),
                 pl.BlockSpec((total, latent_width), lambda i, _: (0, 0)),
                 pl.BlockSpec((latent_width, total), lambda i, _: (0, 0)),
             ],
-            out_specs=pl.BlockSpec((rows, VHEAD), lambda i, _: (0, i)),
+            out_specs=pl.BlockSpec((rows, group * VHEAD), lambda i, _: (0, i)),
             scratch_shapes=[
-                pltpu.VMEM((latent_width, rows), jnp.bfloat16),
+                pltpu.VMEM((group, latent_width, rows), jnp.bfloat16),
+                pltpu.VMEM((total, rows), jnp.float32),
                 pltpu.VMEM((total, rows), jnp.float32),
             ],
         ),
         out_shape=jax.ShapeDtypeStruct((rows, count * VHEAD), jnp.bfloat16),
-        compiler_params=pltpu.CompilerParams(vmem_limit_bytes=48 * 2 ** 20),
+        compiler_params=pltpu.CompilerParams(vmem_limit_bytes=50 * 2 ** 20),
         cost_estimate=pl.CostEstimate(
             flops=4 * count * rows * total * (latent_width + LATENT),
             bytes_accessed=count * (rows * 320 + 2 * NOPE * LATENT) * 2 + 4 * total * latent_width,
             transcendentals=count * rows * total,
         ),
     )(query_start, queries_t, key_absorb, value_absorb, keys, keys_t)
+
+
+def join_kernel(count, *refs):
+    width = refs[0].shape[1]
+    for place in range(count):
+        refs[-1][:, pl.ds(place * width, width)] = refs[place][...]
+
+
+def join(pieces, after):
+    rows, width = pieces[0].shape
+    later = [] if after is None else [after]
+    return pl.pallas_call(
+        functools.partial(join_kernel, len(pieces)),
+        in_specs=[pl.BlockSpec(memory_space=pltpu.VMEM)] * len(pieces)
+        + [pl.BlockSpec(memory_space=pl.ANY)] * len(later),
+        out_specs=pl.BlockSpec(memory_space=pltpu.VMEM),
+        out_shape=jax.ShapeDtypeStruct((rows, width * len(pieces)), jnp.bfloat16),
+    )(*pieces, *later)
+
+
+def project_kernel(added, source_ref, *refs):
+    rows_ref, weight_ref, out_ref, sum_ref = refs[added:]
+    step = pl.program_id(0)
+    product = jnp.dot(rows_ref[...], weight_ref[...], preferred_element_type=jnp.float32)
+
+    @pl.when(step == 0)
+    def _():
+        sum_ref[...] = product + refs[0][...] if added else product
+
+    @pl.when(step > 0)
+    def _():
+        sum_ref[...] += product
+
+    @pl.when(step == pl.num_programs(0) - 1)
+    def _():
+        out_ref[...] = sum_ref[...].astype(out_ref.dtype)
+
+
+def project(so_far, gathered, out_proj, blocks, depth, held_as):
+    rows, columns = gathered.shape[0], out_proj.shape[1]
+    added = so_far is not None
+    whole = pl.BlockSpec((rows, columns), lambda i, _: (0, 0))
+    return pl.pallas_call(
+        functools.partial(project_kernel, int(added)),
+        grid_spec=pltpu.PrefetchScalarGridSpec(
+            num_scalar_prefetch=1,
+            grid=(gathered.shape[1] // depth,),
+            in_specs=[whole] * added
+            + [
+                pl.BlockSpec((rows, depth), lambda i, _: (0, i)),
+                pl.BlockSpec((depth, columns), lambda i, blocks: (blocks[i], 0)),
+            ],
+            out_specs=whole,
+            scratch_shapes=[pltpu.VMEM((rows, columns), jnp.float32)],
+        ),
+        out_shape=jax.ShapeDtypeStruct((rows, columns), held_as),
+        compiler_params=pltpu.CompilerParams(vmem_limit_bytes=40 * 2 ** 20),
+        cost_estimate=pl.CostEstimate(
+            flops=2 * rows * gathered.shape[1] * columns,
+            bytes_accessed=2 * gathered.shape[1] * (rows + columns) + 8 * rows * columns,
+            transcendentals=0,
+        ),
+    )(blocks, *([so_far] * added), gathered, out_proj)
 
 
 def on_device(
@@ -121,37 +201,34 @@
 
     count = local_heads // CHUNKS
     depth = count * VHEAD
-    complete = jnp.zeros((ctx_count * owned, columns), jnp.float32)
-    before = None
+    sources = lax.rem(ep_me + ep_count - jnp.arange(ep_count, dtype=jnp.int32), ep_count)
+    heads = [
+        attention(chunk, count, query_start, queries_t, key_absorb, value_absorb, keys, keys_t)
+        for chunk in range(CHUNKS)
+    ]
+    complete = None
     for chunk in range(CHUNKS):
-        heads = attention(
-            chunk, count, query_start, queries_t, key_absorb, value_absorb, keys, keys_t
-        )
-        pieces = [lax.dynamic_slice_in_dim(heads, ep_me * owned, owned, axis=0)]
+        pieces = [lax.dynamic_slice_in_dim(heads[chunk], ep_me * owned, owned, axis=0)]
         for shift in range(1, ep_count):
             target = lax.rem(ep_me + shift, ep_count)
-            block = lax.dynamic_slice_in_dim(heads, target * owned, owned, axis=0)
+            block = lax.dynamic_slice_in_dim(heads[chunk], target * owned, owned, axis=0)
             pieces.append(
                 lax.ppermute(
                     block, "ep", [(i, (i + shift) % ep_count) for i in range(ep_count)]
                 )
             )
-        mine = jnp.concatenate(pieces, axis=1)
-        if before is not None:
-            mine, before = lax.optimization_barrier((mine, before))
+        last = chunk == CHUNKS - 1
+        mine = join(pieces, None if last else heads[chunk + 1])
         gathered = lax.all_gather(mine, "ctx", axis=0, tiled=True)
-        before = gathered[:8, :128]
-        for shift in range(ep_count):
-            source = lax.rem(ep_me - shift + ep_count, ep_count)
-            weight = lax.dynamic_slice_in_dim(
-                out_proj, source * (local_heads * VHEAD) + chunk * depth, depth, axis=0
-            )
-            complete = complete + jnp.dot(
-                gathered[:, shift * depth : (shift + 1) * depth],
-                weight,
-                preferred_element_type=jnp.float32,
-            )
-    complete = complete.astype(jnp.bfloat16).reshape(ctx_count, -1, columns)
+        complete = project(
+            complete,
+            gathered,
+            out_proj,
+            sources * CHUNKS + chunk,
+            depth,
+            jnp.bfloat16 if last else jnp.float32,
+        )
+    complete = complete.reshape(ctx_count, -1, columns)
     attended = lax.all_to_all(complete, "ctx", split_axis=0, concat_axis=2, tiled=True).reshape(
         -1, columns * ctx_count
     )

time: 367 us -> 347 us (0.946); the launches traced: 366 us -> 341 us
  matrix products: 81 us -> 10.5 us
  local copies, waits for them, and re-layouts: 12.7 us -> 32.1 us
  Pallas kernels: 102 us -> 121 us
  waiting for transfers between devices: 80.2 us -> 94.3 us
  starting transfers between devices: 26.5 us -> 21.6 us
    dot_general x16 -> x0, matrix products: 70.5 us -> none  [on_device(): jnp.dot(gathered[:, shift * depth:(shift + 1) * depth], weight, preferred...]
    pallas_call x0 -> x8, Pallas kernels: none -> 41.7 us  [the longest x4 34 us: project(): pl.pallas_call(functools.partial(project_kernel, int(added)), grid_spec=p...]
    all_gather x4, waiting for transfers between devices: 0.01 us -> 37 us  [on_device(): gathered = lax.all_gather(mine, 'ctx', axis=0, tiled=True)]
    ppermute x12, waiting for transfers between devices: 32.1 us -> 9.16 us  [on_device(): lax.ppermute(block, 'ep', [(i, (i + shift) % ep_count) for i in range(ep_...]
    pallas_call x4, Pallas kernels: 102 us -> 79.1 us  [attention(): pl.pallas_call(attention_kernel, grid_spec=pltpu.PrefetchScalarGridSpec(n...]
    unnamed x43 -> x59, local copies, waits for them, and re-layouts: 8.39 us -> 20.1 us
    dynamic_slice x4, local copies, waits for them, and re-layouts: 0.19 us -> 6.39 us  [on_device(): lax.dynamic_slice_in_dim(heads[chunk], target * owned, owned, axis=0)]
    ppermute x12, starting transfers between devices: 22.6 us -> 17.9 us  [on_device(): lax.ppermute(block, 'ep', [(i, (i + shift) % ep_count) for i in range(ep_...]
  transfers between devices with their start and end apart: 18 -> 18, of which waited for: 11 -> 6; matrix products, arithmetic and copies ran while one was open for 15% -> 2% of each run, Pallas kernels for 21% -> 26%
where the time goes in v2:
time: 347 us; the launch traced here: 341 us
  Pallas kernels  121 us (35%)
  waiting for transfers between devices  94.3 us (27%)
  blocking collectives  44.9 us (13%)
  local copies, waits for them, and re-layouts  32.1 us (9%)
  starting transfers between devices  21.6 us (6%)
  between operations  13.8 us (4%)
  matrix products  10.5 us (3%)
    pallas_call x4, Pallas kernels, attention(): pl.pallas_call(attention_kernel, grid_spec=pltpu.PrefetchScalarGridSpec(n...  79.1 us
    all_gather x4, waiting for transfers between devices, on_device(): gathered = lax.all_gather(mine, 'ctx', axis=0, tiled=True)  37 us
    all_gather x1, waiting for transfers between devices, on_device(): keys = lax.all_gather(latents, 'ctx', axis=0, tiled=True)  34 us
    pallas_call x4, Pallas kernels, project(): pl.pallas_call(functools.partial(project_kernel, int(added)), grid_spec=p...  34 us
    unnamed x59, local copies, waits for them, and re-layouts  20.1 us
    ppermute x12, starting transfers between devices, on_device(): lax.ppermute(block, 'ep', [(i, (i + shift) % ep_count) for i in range(ep_...  17.9 us
    all_to_all x1, blocking collectives, on_device(): lax.all_to_all(partial_out, 'ctx', split_axis=0, concat_axis=0, tiled=True)  16.5 us
    all_to_all x1, waiting for transfers between devices, on_device(): lax.all_to_all(complete, 'ctx', split_axis=0, concat_axis=2, tiled=True)  13.4 us
  transfers between devices with their start and end apart: 18, of which 6 were waited for; matrix products, arithmetic and copies ran while one was open for 2% of the time, Pallas kernels for 26%

profile of v2, /device:TPU:0, one launch (start us, length us, event | category | flops | bytes accessed | tf_op | source)
XLA Modules:
  0.0 340.5 jit_solution(12361569230487972136)
XLA Ops:
  6.5 0.7 all-gather.6.cloned.1.call-update
  7.3 34.0 %all-gather.6.cloned.1.call-done = bf16[2048,576]{0,1:T(8,128)(2,1)} async-done(((bf16[256,576]{0,1:T(8,128)(2,1)}), bf16[2048,576]{0,1:T(8,128)(2,1)}) %all-gather.6.cloned.1.call-update) | async-done | bytes 2359312 | tf_op jit(solution)/shard_map/all_gather | solution.py:198
  41.3 4.6 %copy.28.lat_ref = bf16[2048,576]{1,0:T(8,128)(2,1)} copy(bf16[2048,576]{0,1:T(8,128)(2,1)} %all-gather.6.cloned.1.call-done) | data formatting | bytes 4718592 | tf_op jit(solution)/shard_map/all_gather | solution.py:198
  45.9 19.7 %shard_map.118 = bf16[256,1024]{1,0:T(8,128)(2,1)S(1)} custom-call(s32[1]{0:T(128)} %bitcast.start_ref, bf16[32,192,256]{2,1,0:T(8,128)(2,1)} %bitcast.67, bf16[32,128,512]{2,1,0:T(8,128)(2,1)} %ka_ref.7, bf16[32,512,128]{2,1,0:T(8,128)(2,1)} %va_ref.7, bf16[2048,576]{1,0:T(8,128)(2,1)} %copy.28.lat_ref, bf16[576,2048]{1,0:T(8,128)(2,1)S(1)} %bitcast.61), custom_call_target="tpu_custom_call" | custom-call | flops 18253611008 | bytes 8126464 | tf_op jit(solution)/shard_map/pallas_call | solution.py:83
  65.6 0.7 constant_dynamic-slice_fusion.12
  66.3 3.3 collective-permute-start.2
  69.6 1.6 collective-permute-start
  71.2 19.7 %shard_map.119.refs_4_ = bf16[256,1024]{1,0:T(8,128)(2,1)S(1)} custom-call(s32[1]{0:T(128)} %bitcast.start_ref, bf16[32,192,256]{2,1,0:T(8,128)(2,1)} %bitcast.68, bf16[32,128,512]{2,1,0:T(8,128)(2,1)} %ka_ref.7, bf16[32,512,128]{2,1,0:T(8,128)(2,1)} %va_ref.7, bf16[2048,576]{1,0:T(8,128)(2,1)} %copy.28.lat_ref, bf16[576,2048]{1,0:T(8,128)(2,1)S(1)} %bitcast.62), custom_call_target="tpu_custom_call" | custom-call | flops 18253611008 | bytes 8126464 | tf_op jit(solution)/shard_map/pallas_call | solution.py:83
  91.0 0.8 copy-done.10
  91.8 0.6 copy-done.14
  92.5 1.9 shard_map.120
  94.5 1.8 constant_dynamic-slice_fusion.8
  96.3 2.7 collective-permute-start.5
  99.0 1.1 collective-permute-start.4
  100.1 0.2 collective-permute-start.3
  100.3 20.0 %shard_map.122.refs_4_ = bf16[256,1024]{1,0:T(8,128)(2,1)S(1)} custom-call(s32[1]{0:T(128)} %bitcast.start_ref, bf16[32,192,256]{2,1,0:T(8,128)(2,1)} %bitcast.69, bf16[32,128,512]{2,1,0:T(8,128)(2,1)} %ka_ref.7, bf16[32,512,128]{2,1,0:T(8,128)(2,1)} %va_ref.7, bf16[2048,576]{1,0:T(8,128)(2,1)} %copy.28.lat_ref, bf16[576,2048]{1,0:T(8,128)(2,1)S(1)} %bitcast.63), custom_call_target="tpu_custom_call" | custom-call | flops 18253611008 | bytes 8126464 | tf_op jit(solution)/shard_map/pallas_call | solution.py:83
  120.3 0.8 copy-done.11
  121.1 0.6 copy-done.15
  121.9 1.9 shard_map.123
  123.9 1.9 constant_dynamic-slice_fusion.4
  125.7 3.8 %collective-permute-start.8 = (bf16[64,1024]{1,0:T(8,128)(2,1)S(1)}, bf16[64,1024]{1,0:T(8,128)(2,1)S(1)}, u32[]{:S(2)}, u32[]{:S(2)}) collective-permute-start(bf16[64,1024]{1,0:T(8,128)(2,1)S(1)} %get-tuple-element.13), channel_id=1, source_target_pairs={{0,3},{1,0},{2,1},{3,2},{4,7},{5,4},{6,5},{7,6},{8,11},{9,8},{10,9... | collective-permute-start | bytes 393224 | tf_op jit(solution)/shard_map/ppermute | solution.py:216
  129.5 0.8 collective-permute-start.6
  130.3 19.7 %shard_map.125.refs_4_ = bf16[256,1024]{1,0:T(8,128)(2,1)S(1)} custom-call(s32[1]{0:T(128)} %bitcast.start_ref, bf16[32,192,256]{2,1,0:T(8,128)(2,1)} %bitcast.70, bf16[32,128,512]{2,1,0:T(8,128)(2,1)} %ka_ref.7, bf16[32,512,128]{2,1,0:T(8,128)(2,1)} %va_ref.7, bf16[2048,576]{1,0:T(8,128)(2,1)} %copy.28.lat_ref, bf16[576,2048]{1,0:T(8,128)(2,1)S(1)} %bitcast.64), custom_call_target="tpu_custom_call" | custom-call | flops 18253611008 | bytes 8126464 | tf_op jit(solution)/shard_map/pallas_call | solution.py:83
  150.0 0.8 copy-done.9
  150.8 0.6 copy-done.13
  151.6 1.9 shard_map.126
  153.6 2.0 constant_dynamic-slice_fusion
  155.6 3.0 collective-permute-start.11
  158.6 1.1 collective-permute-start.10
  159.7 0.3 collective-permute-start.9
  160.0 3.1 collective-permute-done.11.refs_3_
  163.2 6.0 %collective-permute-done.10.refs_2_ = bf16[64,1024]{1,0:T(8,128)(2,1)S(1)} collective-permute-done((bf16[64,1024]{1,0:T(8,128)(2,1)S(1)}, bf16[64,1024]{1,0:T(8,128)(2,1)S(1)}, u32[]{:S(2)}, u32[]{:S(2)}) %collective-permute-start.10) | collective-permute-done | bytes 131104 | tf_op jit(solution)/shard_map/ppermute | solution.py:216
  169.2 0.6 copy-done.23
  169.9 1.9 shard_map.128
  172.1 1.2 reduce-window.6
  173.3 0.2 slice_reduce_fusion
  173.9 2.2 copy-done.4
  176.1 8.3 %shard_map.121.refs_0_ = f32[512,896]{1,0:T(8,128)S(1)} custom-call(s32[4]{0:T(128)S(1)} %fusion.34.source_ref, bf16[512,4096]{1,0:T(8,128)(2,1)S(1)} %copy-done.4, bf16[16384,896]{1,0:T(8,128)(2,1)} %refs_2_.5), custom_call_target="tpu_custom_call" | custom-call | flops 3758096384 | bytes 15204352 | tf_op jit(solution)/shard_map/pallas_call | solution.py:152
  184.3 1.2 copy-done.2
  185.6 1.5 copy-done.3
  187.1 2.2 copy-done.5
  189.3 8.2 %shard_map.124.refs_0_ = f32[512,896]{1,0:T(8,128)S(1)} custom-call(s32[4]{0:T(128)S(1)} %broadcast_add_fusion.source_ref, f32[512,896]{1,0:T(8,128)S(1)} %copy-done.3, bf16[512,4096]{1,0:T(8,128)(2,1)S(1)} %copy-done.5, bf16[16384,896]{1,0:T(8,128)(2,1)} %refs_2_.5), custom_call_target="tpu_custom_call" | custom-call | flops 3758096384 | bytes 15204352 | tf_op jit(solution)/shard_map/pallas_call | solution.py:152
  197.5 10.3 %all-gather.12.cloned.1.call-done.refs_1_ = bf16[512,4096]{1,0:T(8,128)(2,1)} async-done(((bf16[64,4096]{1,0:T(8,128)(2,1)}), bf16[512,4096]{1,0:T(8,128)(2,1)}) %all-gather.12.cloned.1.call-update) | async-done | bytes 4194320 | tf_op jit(solution)/shard_map/all_gather | solution.py:222
  207.8 2.2 copy-done.6
  210.0 8.4 %shard_map.127.refs_0_ = f32[512,896]{1,0:T(8,128)S(1)} custom-call(s32[4]{0:T(128)S(1)} %broadcast_add_fusion.1.source_ref, f32[512,896]{1,0:T(8,128)S(1)} %shard_map.124.refs_0_, bf16[512,4096]{1,0:T(8,128)(2,1)S(1)} %copy-done.6, bf16[16384,896]{1,0:T(8,128)(2,1)} %refs_2_.5), custom_call_target="tpu_custom_call" | custom-call | flops 3758096384 | bytes 15204352 | tf_op jit(solution)/shard_map/pallas_call | solution.py:152
  218.4 1.2 copy-done
  219.7 26.7 %all-gather.14.cloned.1.call-done.refs_1_ = bf16[512,4096]{1,0:T(8,128)(2,1)} async-done(((bf16[64,4096]{1,0:T(8,128)(2,1)}), bf16[512,4096]{1,0:T(8,128)(2,1)}) %all-gather.14.cloned.1.call-update) | async-done | bytes 4194320 | tf_op jit(solution)/shard_map/all_gather | solution.py:222
  246.3 1.5 copy-done.1
  247.8 2.2 copy-done.7
  250.0 9.1 %shard_map.129 = bf16[512,896]{1,0:T(8,128)(2,1)} custom-call(s32[4]{0:T(128)S(1)} %broadcast_add_fusion.2.source_ref, f32[512,896]{1,0:T(8,128)S(1)} %copy-done.1, bf16[512,4096]{1,0:T(8,128)(2,1)S(1)} %copy-done.7, bf16[16384,896]{1,0:T(8,128)(2,1)} %refs_2_.5), custom_call_target="tpu_custom_call" | custom-call | flops 3758096384 | bytes 15204352 | tf_op jit(solution)/shard_map/pallas_call | solution.py:152
  259.1 3.6 %all-to-all-start = ((bf16[8,64,896]{2,1,0:T(8,128)(2,1)}), bf16[8,64,896]{2,1,0:T(8,128)(2,1)S(1)}, u32[]{:S(2)}, u32[]{:S(2)}) async-start(bf16[8,64,896]{2,1,0:T(8,128)(2,1)} %bitcast.3), calls=%async_computation | async-start | bytes 1835008 | tf_op jit(solution)/shard_map/all_to_all | solution.py:232
  263.0 0.2 fusion.36
  263.2 13.4 %all-to-all-done = bf16[8,64,896]{2,1,0:T(8,128)(2,1)S(1)} async-done(((bf16[8,64,896]{2,1,0:T(8,128)(2,1)}), bf16[8,64,896]{2,1,0:T(8,128)(2,1)S(1)}, u32[]{:S(2)}, u32[]{:S(2)}) %all-to-all-start) | async-done | bytes 917536 | tf_op jit(solution)/shard_map/all_to_all | solution.py:232
  276.9 0.4 fusion.7
  277.3 0.3 copy-done.27
  277.7 0.4 convolution_convert_fusion.1
  278.1 10.3 %all_to_all.24 = bf16[4,2,7168]{2,1,0:T(2,128)(2,1)S(1)} all-to-all(bf16[4,2,7168]{2,1,0:T(2,128)(2,1)S(1)} %reshape.109), channel_id=1, replica_groups=mesh['ctx'=8,'ep'=4] {'ep'}, dimensions={0} | all-to-all | bytes 229376 | tf_op jit(solution)/shard_map/all_to_all | solution.py:256
  288.4 9.7 %all_gather.23 = bf16[32,2,7168]{2,1,0:T(2,128)(2,1)S(1)} all-gather(bf16[4,2,7168]{2,1,0:T(2,128)(2,1)S(1)} %all_to_all.24), channel_id=1, replica_groups=mesh['ctx'=8,'ep'=4] {'ctx'}, dimensions={0}, use_global_device_ids=true | all-gather | bytes 1032192 | tf_op jit(solution)/shard_map/all_gather | solution.py:261
  298.1 0.3 reshape.110
  298.4 2.8 fusion.5
  301.2 5.5 %fusion.1 = bf16[8,8,7168]{2,1,0:T(8,128)(2,1)S(1)} fusion(bf16[1,256,7168]{2,1,0:T(8,128)(2,1)} %param.21, bf16[64,7168]{1,0:T(8,128)(2,1)S(1)} %reshape.110, bf16[1,7168,256]{2,1,0:T(8,128)(2,1)} %param.20, f32[64,256]{1,0:T(8,128)S(1)} %fusion.5), kind=kOutput, calls=%fused_computation.3 | convolution fusion | flops 470319104 | bytes 9240576 | tf_op jit(solution)/shard_map/dot_general | solution.py:267
  306.6 16.5 %all_to_all.25 = bf16[8,8,7168]{2,1,0:T(8,128)(2,1)S(1)} all-to-all(bf16[8,8,7168]{2,1,0:T(8,128)(2,1)S(1)} %fusion.1), channel_id=1, replica_groups=mesh['ctx'=8,'ep'=4] {'ctx'}, dimensions={0} | all-to-all | bytes 1835008 | tf_op jit(solution)/shard_map/all_to_all | solution.py:269
  323.4 8.4 %all_to_all.26 = bf16[4,2,7168]{2,1,0:T(2,128)(2,1)S(1)} all-to-all(bf16[4,2,7168]{2,1,0:T(2,128)(2,1)S(1)} %reshape.112), channel_id=1, replica_groups=mesh['ctx'=8,'ep'=4] {'ep'}, dimensions={0} | all-to-all | bytes 229376 | tf_op jit(solution)/shard_map/all_to_all | solution.py:272
  331.8 1.9 fusion
  (86 shorter events, 2.2 us)
Async XLA Ops:
  6.5 34.8 %all-gather.6.cloned.1.call-start = ((), (), s32[]{:S(2)}) async-start(), calls=%async_computation.4 | async-start | bytes 2654208 | tf_op jit(solution)/shard_map/all_gather | solution.py:198
  7.3 166.6 %all-gather.8.cloned.1.call-start = ((), (), s32[]{:S(2)}) async-start(), calls=%async_computation.5 | async-start | bytes 4718592 | tf_op jit(solution)/shard_map/all_gather | solution.py:222
  41.3 4.6 %copy-start.8 = (bf16[2048,576]{0,1:T(8,128)(2,1)S(1)}, bf16[2048,576]{0,1:T(8,128)(2,1)}, u32[]{:S(2)}) copy-start(bf16[2048,576]{0,1:T(8,128)(2,1)} %all-gather.6.cloned.1.call-done) | copy-start | bytes 7077892
  66.3 25.5 %collective-permute-start.2 = (bf16[64,1024]{1,0:T(8,128)(2,1)S(1)}, bf16[64,1024]{1,0:T(8,128)(2,1)S(1)}, u32[]{:S(2)}, u32[]{:S(2)}) collective-permute-start(bf16[64,1024]{1,0:T(8,128)(2,1)S(1)} %get-tuple-element.21), channel_id=1, source_target_pairs={{0,3},{1,0},{2,1},{3,2},{4,7},{5,4},{6,5},{7,6},{8,11},{9,8},{10,9... | collective-permute-start | bytes 393224 | tf_op jit(solution)/shard_map/ppermute | solution.py:216
  69.6 22.1 %collective-permute-start.1 = (bf16[64,1024]{1,0:T(8,128)(2,1)S(1)}, bf16[64,1024]{1,0:T(8,128)(2,1)S(1)}, u32[]{:S(2)}, u32[]{:S(2)}) collective-permute-start(bf16[64,1024]{1,0:T(8,128)(2,1)S(1)} %get-tuple-element.22), channel_id=1, source_target_pairs={{0,2},{1,3},{2,0},{3,1},{4,6},{5,7},{6,4},{7,5},{8,10},{9,11},{10,... | collective-permute-start | bytes 393224 | tf_op jit(solution)/shard_map/ppermute | solution.py:216
  69.6 22.1 %collective-permute-start = (bf16[64,1024]{1,0:T(8,128)(2,1)S(1)}, bf16[64,1024]{1,0:T(8,128)(2,1)S(1)}, u32[]{:S(2)}, u32[]{:S(2)}) collective-permute-start(bf16[64,1024]{1,0:T(8,128)(2,1)S(1)} %get-tuple-element.23), channel_id=1, source_target_pairs={{0,1},{1,2},{2,3},{3,0},{4,5},{5,6},{6,7},{7,4},{8,9},{9,10},{10,1... | collective-permute-start | bytes 393224 | tf_op jit(solution)/shard_map/ppermute | solution.py:216
  90.9 0.8 copy-start.10
  91.7 0.6 copy-start.14
  91.8 0.7 copy-start.17
  91.8 0.7 copy-start.20
  94.4 91.2 %all-gather.10.cloned.1.call-start = ((), (), s32[]{:S(2)}) async-start(), calls=%async_computation.6 | async-start | bytes 4718592 | tf_op jit(solution)/shard_map/all_gather | solution.py:222
  96.3 24.8 %collective-permute-start.5 = (bf16[64,1024]{1,0:T(8,128)(2,1)S(1)}, bf16[64,1024]{1,0:T(8,128)(2,1)S(1)}, u32[]{:S(2)}, u32[]{:S(2)}) collective-permute-start(bf16[64,1024]{1,0:T(8,128)(2,1)S(1)} %get-tuple-element.17), channel_id=1, source_target_pairs={{0,3},{1,0},{2,1},{3,2},{4,7},{5,4},{6,5},{7,6},{8,11},{9,8},{10,9... | collective-permute-start | bytes 393224 | tf_op jit(solution)/shard_map/ppermute | solution.py:216
  99.0 22.1 %collective-permute-start.4 = (bf16[64,1024]{1,0:T(8,128)(2,1)S(1)}, bf16[64,1024]{1,0:T(8,128)(2,1)S(1)}, u32[]{:S(2)}, u32[]{:S(2)}) collective-permute-start(bf16[64,1024]{1,0:T(8,128)(2,1)S(1)} %get-tuple-element.18), channel_id=1, source_target_pairs={{0,2},{1,3},{2,0},{3,1},{4,6},{5,7},{6,4},{7,5},{8,10},{9,11},{10,... | collective-permute-start | bytes 393224 | tf_op jit(solution)/shard_map/ppermute | solution.py:216
  100.1 21.0 %collective-permute-start.3 = (bf16[64,1024]{1,0:T(8,128)(2,1)S(1)}, bf16[64,1024]{1,0:T(8,128)(2,1)S(1)}, u32[]{:S(2)}, u32[]{:S(2)}) collective-permute-start(bf16[64,1024]{1,0:T(8,128)(2,1)S(1)} %get-tuple-element.19), channel_id=1, source_target_pairs={{0,1},{1,2},{2,3},{3,0},{4,5},{5,6},{6,7},{7,4},{8,9},{9,10},{10,1... | collective-permute-start | bytes 393224 | tf_op jit(solution)/shard_map/ppermute | solution.py:216
  120.3 0.8 copy-start.11
  121.1 0.6 copy-start.15
  121.1 0.7 copy-start.18
  121.1 0.7 copy-start.21
  123.8 84.0 %all-gather.12.cloned.1.call-start = ((), (), s32[]{:S(2)}) async-start(), calls=%async_computation.7 | async-start | bytes 4718592 | tf_op jit(solution)/shard_map/all_gather | solution.py:222
  125.7 25.0 %collective-permute-start.8 = (bf16[64,1024]{1,0:T(8,128)(2,1)S(1)}, bf16[64,1024]{1,0:T(8,128)(2,1)S(1)}, u32[]{:S(2)}, u32[]{:S(2)}) collective-permute-start(bf16[64,1024]{1,0:T(8,128)(2,1)S(1)} %get-tuple-element.13), channel_id=1, source_target_pairs={{0,3},{1,0},{2,1},{3,2},{4,7},{5,4},{6,5},{7,6},{8,11},{9,8},{10,9... | collective-permute-start | bytes 393224 | tf_op jit(solution)/shard_map/ppermute | solution.py:216
  129.5 21.3 %collective-permute-start.7 = (bf16[64,1024]{1,0:T(8,128)(2,1)S(1)}, bf16[64,1024]{1,0:T(8,128)(2,1)S(1)}, u32[]{:S(2)}, u32[]{:S(2)}) collective-permute-start(bf16[64,1024]{1,0:T(8,128)(2,1)S(1)} %get-tuple-element.14), channel_id=1, source_target_pairs={{0,2},{1,3},{2,0},{3,1},{4,6},{5,7},{6,4},{7,5},{8,10},{9,11},{10,... | collective-permute-start | bytes 393224 | tf_op jit(solution)/shard_map/ppermute | solution.py:216
  129.5 21.3 %collective-permute-start.6 = (bf16[64,1024]{1,0:T(8,128)(2,1)S(1)}, bf16[64,1024]{1,0:T(8,128)(2,1)S(1)}, u32[]{:S(2)}, u32[]{:S(2)}) collective-permute-start(bf16[64,1024]{1,0:T(8,128)(2,1)S(1)} %get-tuple-element.15), channel_id=1, source_target_pairs={{0,1},{1,2},{2,3},{3,0},{4,5},{5,6},{6,7},{7,4},{8,9},{9,10},{10,1... | collective-permute-start | bytes 393224 | tf_op jit(solution)/shard_map/ppermute | solution.py:216
  150.0 0.8 copy-start.9
  150.8 21.0 %copy-start.25 = (s32[64,8]{0,1:T(8,128)S(1)}, s32[64,8]{0,1:T(8,128)}, u32[]{:S(2)}) copy-start(s32[64,8]{0,1:T(8,128)} %param.22) | copy-start | bytes 6148
  150.8 0.7 copy-start.13
  150.8 0.7 copy-start.16
  150.8 0.8 copy-start.19
  153.5 92.8 %all-gather.14.cloned.1.call-start = ((), (), s32[]{:S(2)}) async-start(), calls=%async_computation.8 | async-start | bytes 4718592 | tf_op jit(solution)/shard_map/all_gather | solution.py:222
  155.6 7.6 %collective-permute-start.11 = (bf16[64,1024]{1,0:T(8,128)(2,1)S(1)}, bf16[64,1024]{1,0:T(8,128)(2,1)S(1)}, u32[]{:S(2)}, u32[]{:S(2)}) collective-permute-start(bf16[64,1024]{1,0:T(8,128)(2,1)S(1)} %get-tuple-element.9), channel_id=1, source_target_pairs={{0,3},{1,0},{2,1},{3,2},{4,7},{5,4},{6,5},{7,6},{8,11},{9,8},{10,9... | collective-permute-start | bytes 393224 | tf_op jit(solution)/shard_map/ppermute | solution.py:216
  158.6 10.5 %collective-permute-start.10 = (bf16[64,1024]{1,0:T(8,128)(2,1)S(1)}, bf16[64,1024]{1,0:T(8,128)(2,1)S(1)}, u32[]{:S(2)}, u32[]{:S(2)}) collective-permute-start(bf16[64,1024]{1,0:T(8,128)(2,1)S(1)} %get-tuple-element.10), channel_id=1, source_target_pairs={{0,2},{1,3},{2,0},{3,1},{4,6},{5,7},{6,4},{7,5},{8,10},{9,11},{10,... | collective-permute-start | bytes 393224 | tf_op jit(solution)/shard_map/ppermute | solution.py:216
  159.7 9.4 %collective-permute-start.9 = (bf16[64,1024]{1,0:T(8,128)(2,1)S(1)}, bf16[64,1024]{1,0:T(8,128)(2,1)S(1)}, u32[]{:S(2)}, u32[]{:S(2)}) collective-permute-start(bf16[64,1024]{1,0:T(8,128)(2,1)S(1)} %get-tuple-element.11), channel_id=1, source_target_pairs={{0,1},{1,2},{2,3},{3,0},{4,5},{5,6},{6,7},{7,4},{8,9},{9,10},{10,1... | collective-permute-start | bytes 393224 | tf_op jit(solution)/shard_map/ppermute | solution.py:216
  163.2 6.0 %copy-start.22 = (bf16[64,1024]{1,0:T(8,128)(2,1)}, bf16[64,1024]{1,0:T(8,128)(2,1)S(1)}, u32[]{:S(2)}) copy-start(bf16[64,1024]{1,0:T(8,128)(2,1)S(1)} %collective-permute-done.11.refs_3_) | copy-start | bytes 393220
  169.2 0.7 copy-start.23
  169.2 0.7 copy-start.24
  173.9 2.2 copy-start.4
  184.3 1.2 copy-start.2
  185.6 1.5 copy-start.3
  187.1 2.2 copy-start.5
  207.8 2.2 copy-start.6
  218.4 1.2 copy-start
  246.3 1.5 copy-start.1
  247.8 2.2 copy-start.7
  250.0 12.7 %copy-start.26 = (f32[64,8]{0,1:T(8,128)S(1)}, f32[64,8]{0,1:T(8,128)}, u32[]{:S(2)}) copy-start(f32[64,8]{0,1:T(8,128)} %param.23) | copy-start | bytes 6148
  259.1 17.5 %all-to-all-start = ((bf16[8,64,896]{2,1,0:T(8,128)(2,1)}), bf16[8,64,896]{2,1,0:T(8,128)(2,1)S(1)}, u32[]{:S(2)}, u32[]{:S(2)}) async-start(bf16[8,64,896]{2,1,0:T(8,128)(2,1)} %bitcast.3), calls=%async_computation | async-start | bytes 1835008 | tf_op jit(solution)/shard_map/all_to_all | solution.py:232
  263.2 13.7 %copy-start.12 = (bf16[64,7168]{1,0:T(8,128)(2,1)S(1)}, bf16[64,7168]{1,0:T(8,128)(2,1)}, u32[]{:S(2)}) copy-start(bf16[64,7168]{1,0:T(8,128)(2,1)} %param.17) | copy-start | bytes 2752516
  276.9 0.8 copy-start.27
Sparse Core Ops, SparseCore 0:
  9.2 32.0 all-gather.5
  94.5 36.0 all-gather.7
  132.6 36.7 all-gather.9
  171.1 36.7 all-gather.11
  209.6 36.7 all-gather.13

commit v3 on v2

--- a/solution.py
+++ b/solution.py
@@ -13,9 +13,8 @@
 VHEAD = 128
 TOPK = 8
 CAP = 2
-CHUNKS = 4
+EIGHTHS = (3, 1, 4)
 KEY_BLOCK = 256
-GROUP = 4
 LOG2E = 1.4426950408889634
 
 
@@ -71,11 +70,11 @@
         highest = jnp.max(top, axis=0, keepdims=True)
 
 
-def attention(chunk, count, query_start, queries_t, key_absorb, value_absorb, keys, keys_t):
+def attention(first_head, count, query_start, queries_t, key_absorb, value_absorb, keys, keys_t):
     _, width, rows = queries_t.shape
     total, latent_width = keys.shape
-    group = GROUP if count % GROUP == 0 else 1
-    first = chunk * count // group
+    group = next(size for size in (4, 2, 1) if count % size == 0 and first_head % size == 0)
+    first = first_head // group
 
     def by_head(i, _):
         return (first + i, 0, 0)
@@ -110,20 +109,23 @@
 
 
 def join_kernel(count, *refs):
-    width = refs[0].shape[1]
+    begin = 0
     for place in range(count):
-        refs[-1][:, pl.ds(place * width, width)] = refs[place][...]
+        width = refs[place].shape[1]
+        refs[-1][:, pl.ds(begin, width)] = refs[place][...]
+        begin += width
 
 
 def join(pieces, after):
-    rows, width = pieces[0].shape
+    rows = pieces[0].shape[0]
+    width = sum(piece.shape[1] for piece in pieces)
     later = [] if after is None else [after]
     return pl.pallas_call(
         functools.partial(join_kernel, len(pieces)),
         in_specs=[pl.BlockSpec(memory_space=pltpu.VMEM)] * len(pieces)
         + [pl.BlockSpec(memory_space=pl.ANY)] * len(later),
         out_specs=pl.BlockSpec(memory_space=pltpu.VMEM),
-        out_shape=jax.ShapeDtypeStruct((rows, width * len(pieces)), jnp.bfloat16),
+        out_shape=jax.ShapeDtypeStruct((rows, width), jnp.bfloat16),
     )(*pieces, *later)
 
 
@@ -163,7 +165,7 @@
             scratch_shapes=[pltpu.VMEM((rows, columns), jnp.float32)],
         ),
         out_shape=jax.ShapeDtypeStruct((rows, columns), held_as),
-        compiler_params=pltpu.CompilerParams(vmem_limit_bytes=40 * 2 ** 20),
+        compiler_params=pltpu.CompilerParams(vmem_limit_bytes=56 * 2 ** 20),
         cost_estimate=pl.CostEstimate(
             flops=2 * rows * gathered.shape[1] * columns,
             bytes_accessed=2 * gathered.shape[1] * (rows + columns) + 8 * rows * columns,
@@ -199,34 +201,46 @@
     keys_t = keys.T
     queries_t = jnp.transpose(queries, (1, 2, 0))
 
-    count = local_heads // CHUNKS
-    depth = count * VHEAD
-    sources = lax.rem(ep_me + ep_count - jnp.arange(ep_count, dtype=jnp.int32), ep_count)
-    heads = [
-        attention(chunk, count, query_start, queries_t, key_absorb, value_absorb, keys, keys_t)
-        for chunk in range(CHUNKS)
-    ]
+    unit = local_heads // 8
+    depth = unit * VHEAD
+    heads, starts = [], []
+    for part in EIGHTHS:
+        starts.append(sum(EIGHTHS[: len(starts)]))
+        heads.append(
+            attention(
+                starts[-1] * unit,
+                part * unit,
+                query_start,
+                queries_t,
+                key_absorb,
+                value_absorb,
+                keys,
+                keys_t,
+            )
+        )
     complete = None
-    for chunk in range(CHUNKS):
-        pieces = [lax.dynamic_slice_in_dim(heads[chunk], ep_me * owned, owned, axis=0)]
-        for shift in range(1, ep_count):
-            target = lax.rem(ep_me + shift, ep_count)
-            block = lax.dynamic_slice_in_dim(heads[chunk], target * owned, owned, axis=0)
-            pieces.append(
-                lax.ppermute(
-                    block, "ep", [(i, (i + shift) % ep_count) for i in range(ep_count)]
-                )
-            )
-        last = chunk == CHUNKS - 1
-        mine = join(pieces, None if last else heads[chunk + 1])
-        gathered = lax.all_gather(mine, "ctx", axis=0, tiled=True)
+    for members, after in (((0,), heads[1]), ((1, 2), None)):
+        pieces, blocks = [], []
+        for member in members:
+            for shift in range(ep_count):
+                target = lax.rem(ep_me + shift, ep_count)
+                source = lax.rem(ep_me - shift + ep_count, ep_count)
+                block = lax.dynamic_slice_in_dim(heads[member], target * owned, owned, axis=0)
+                if shift > 0:
+                    block = lax.ppermute(
+                        block, "ep", [(i, (i + shift) % ep_count) for i in range(ep_count)]
+                    )
+                pieces.append(block)
+                for at in range(EIGHTHS[member]):
+                    blocks.append(source * 8 + starts[member] + at)
+        gathered = lax.all_gather(join(pieces, after), "ctx", axis=0, tiled=True)
         complete = project(
             complete,
             gathered,
             out_proj,
-            sources * CHUNKS + chunk,
+            jnp.stack(blocks).astype(jnp.int32),
             depth,
-            jnp.bfloat16 if last else jnp.float32,
+            jnp.float32 if complete is None else jnp.bfloat16,
         )
     complete = complete.reshape(ctx_count, -1, columns)
     attended = lax.all_to_all(complete, "ctx", split_axis=0, concat_axis=2, tiled=True).reshape(

time: 347 us -> 344 us (level); the launches traced: 341 us -> 343 us
  local copies, waits for them, and re-layouts: 32.1 us -> 12.1 us
  waiting for transfers between devices: 94.3 us -> 109 us
  starting transfers between devices: 21.6 us -> 26.7 us
    unnamed x59 -> x35, local copies, waits for them, and re-layouts: 20.1 us -> 2.98 us
    pallas_call x4 -> x2, Pallas kernels: 34 us -> 43.2 us  [project(): pl.pallas_call(functools.partial(project_kernel, int(added)), grid_spec=p...]
    ppermute x12 -> x9, waiting for transfers between devices: 9.16 us -> 18.3 us  [on_device(): lax.ppermute(block, 'ep', [(i, (i + shift) % ep_count) for i in range(ep_...]
    all_gather x4 -> x2, waiting for transfers between devices: 37 us -> 42.2 us  [on_device(): gathered = lax.all_gather(join(pieces, after), 'ctx', axis=0, tiled=True)]
    ppermute x12 -> x9, starting transfers between devices: 17.9 us -> 22.8 us  [on_device(): lax.ppermute(block, 'ep', [(i, (i + shift) % ep_count) for i in range(ep_...]
    dynamic_slice x4 -> x3, local copies, waits for them, and re-layouts: 6.39 us -> 2.18 us  [on_device(): lax.dynamic_slice_in_dim(heads[member], target * owned, owned, axis=0)]
    pallas_call x4 -> x2, Pallas kernels: 7.69 us -> 4.62 us  [join(): pl.pallas_call(functools.partial(join_kernel, len(pieces)), in_specs=[pl....]
    pallas_call x4 -> x3, Pallas kernels: 79.1 us -> 76.3 us  [attention(): pl.pallas_call(attention_kernel, grid_spec=pltpu.PrefetchScalarGridSpec(n...]
  transfers between devices with their start and end apart: 18 -> 13, of which waited for: 6 -> 7; matrix products, arithmetic and copies ran while one was open for 2% -> 2% of each run, Pallas kernels for 26% -> 20%
where the time goes in v3:
time: 344 us; the launch traced here: 343 us
  Pallas kernels  124 us (36%)
  waiting for transfers between devices  109 us (32%)
  blocking collectives  45.2 us (13%)
  starting transfers between devices  26.7 us (8%)
  between operations  13.4 us (4%)
  local copies, waits for them, and re-layouts  12.1 us (4%)
  matrix products  10.5 us (3%)
    pallas_call x3, Pallas kernels, attention(): pl.pallas_call(attention_kernel, grid_spec=pltpu.PrefetchScalarGridSpec(n...  76.3 us
    pallas_call x2, Pallas kernels, project(): pl.pallas_call(functools.partial(project_kernel, int(added)), grid_spec=p...  43.2 us
    all_gather x2, waiting for transfers between devices, on_device(): gathered = lax.all_gather(join(pieces, after), 'ctx', axis=0, tiled=True)  42.2 us
    all_gather x1, waiting for transfers between devices, on_device(): keys = lax.all_gather(latents, 'ctx', axis=0, tiled=True)  34 us
    ppermute x9, starting transfers between devices, on_device(): lax.ppermute(block, 'ep', [(i, (i + shift) % ep_count) for i in range(ep_...  22.8 us
    ppermute x9, waiting for transfers between devices, on_device(): lax.ppermute(block, 'ep', [(i, (i + shift) % ep_count) for i in range(ep_...  18.3 us
    all_to_all x1, blocking collectives, on_device(): lax.all_to_all(partial_out, 'ctx', split_axis=0, concat_axis=0, tiled=True)  16.5 us
    all_to_all x1, waiting for transfers between devices, on_device(): lax.all_to_all(complete, 'ctx', split_axis=0, concat_axis=2, tiled=True)  13.4 us
  transfers between devices with their start and end apart: 13, of which 7 were waited for; matrix products, arithmetic and copies ran while one was open for 2% of the time, Pallas kernels for 20%

profile of v3, /device:TPU:0, one launch (start us, length us, event | category | flops | bytes accessed | tf_op | source)
XLA Modules:
  0.0 342.9 jit_solution(9761883243737592176)
XLA Ops:
  6.5 0.7 all-gather.4.cloned.1.call-update
  7.3 0.0 all-gather.6.cloned.1.call-start
  7.3 34.0 %all-gather.4.cloned.1.call-done = bf16[2048,576]{0,1:T(8,128)(2,1)} async-done(((bf16[256,576]{0,1:T(8,128)(2,1)}), bf16[2048,576]{0,1:T(8,128)(2,1)}) %all-gather.4.cloned.1.call-update) | async-done | bytes 2359312 | tf_op jit(solution)/shard_map/all_gather | solution.py:200
  41.3 4.5 %copy.26.lat_ref = bf16[2048,576]{1,0:T(8,128)(2,1)} copy(bf16[2048,576]{0,1:T(8,128)(2,1)} %all-gather.4.cloned.1.call-done) | data formatting | bytes 4718592 | tf_op jit(solution)/shard_map/all_gather | solution.py:200
  45.8 28.4 %shard_map.118 = bf16[256,1536]{1,0:T(8,128)(2,1)S(1)} custom-call(s32[1]{0:T(128)} %bitcast.32.start_ref, bf16[32,192,256]{2,1,0:T(8,128)(2,1)} %bitcast.99, bf16[32,128,512]{2,1,0:T(8,128)(2,1)} %ka_ref.5, bf16[32,512,128]{2,1,0:T(8,128)(2,1)} %va_ref.5, bf16[2048,576]{1,0:T(8,128)(2,1)} %copy.26.lat_ref, bf16[576,2048]{1,0:T(8,128)(2,1)S(1)} %bitcast.93), custom_call_target="tpu_custom_call" | custom-call | flops 27380416512 | bytes 9830400 | tf_op jit(solution)/shard_map/pallas_call | solution.py:82
  74.2 0.8 constant_dynamic-slice_fusion.8
  75.0 3.3 collective-permute-start.2
  78.3 1.1 collective-permute-start
  79.4 10.8 %shard_map.119.refs_4_ = bf16[256,512]{1,0:T(8,128)(2,1)S(1)} custom-call(s32[1]{0:T(128)} %bitcast.32.start_ref, bf16[32,192,256]{2,1,0:T(8,128)(2,1)} %bitcast.100, bf16[32,128,512]{2,1,0:T(8,128)(2,1)} %ka_ref.5, bf16[32,512,128]{2,1,0:T(8,128)(2,1)} %va_ref.5, bf16[2048,576]{1,0:T(8,128)(2,1)} %copy.26.lat_ref, bf16[576,2048]{1,0:T(8,128)(2,1)S(1)} %bitcast.94), custom_call_target="tpu_custom_call" | custom-call | flops 9126805504 | bytes 6422528 | tf_op jit(solution)/shard_map/pallas_call | solution.py:82
  90.3 0.7 copy-done.1
  91.0 4.6 %collective-permute-done.1.refs_2_ = bf16[64,1536]{1,0:T(8,128)(2,1)S(1)} collective-permute-done((bf16[64,1536]{1,0:T(8,128)(2,1)S(1)}, bf16[64,1536]{1,0:T(8,128)(2,1)S(1)}, u32[]{:S(2)}, u32[]{:S(2)}) %collective-permute-start.1) | collective-permute-done | bytes 196640 | tf_op jit(solution)/shard_map/ppermute | solution.py:230
  95.6 0.7 copy-done.8
  96.3 0.1 copy-done.9
  96.4 2.1 shard_map.120
  98.5 0.0 all-gather.6.cloned.1.call-update
  98.5 0.3 all-gather.8.cloned.1.call-start
  98.8 37.1 %shard_map.122 = bf16[256,2048]{1,0:T(8,128)(2,1)S(1)} custom-call(s32[1]{0:T(128)} %bitcast.32.start_ref, bf16[32,192,256]{2,1,0:T(8,128)(2,1)} %bitcast.101, bf16[32,128,512]{2,1,0:T(8,128)(2,1)} %ka_ref.5, bf16[32,512,128]{2,1,0:T(8,128)(2,1)} %va_ref.5, bf16[2048,576]{1,0:T(8,128)(2,1)} %copy.26.lat_ref, bf16[576,2048]{1,0:T(8,128)(2,1)S(1)} %bitcast.95), custom_call_target="tpu_custom_call" | custom-call | flops 36507222016 | bytes 11534336 | tf_op jit(solution)/shard_map/pallas_call | solution.py:82
  135.9 0.8 constant_dynamic-slice_fusion
  136.7 0.1 collective-permute-start.8
  136.8 2.5 collective-permute-start.7
  139.3 2.0 collective-permute-start.6
  141.3 0.6 constant_dynamic-slice_fusion.4
  142.0 1.8 collective-permute-start.5
  143.8 11.8 %collective-permute-done.5.refs_3_ = bf16[64,512]{1,0:T(8,128)(2,1)S(1)} collective-permute-done((bf16[64,512]{1,0:T(8,128)(2,1)S(1)}, bf16[64,512]{1,0:T(8,128)(2,1)S(1)}, u32[]{:S(2)}, u32[]{:S(2)}) %collective-permute-start.5) | collective-permute-done | bytes 65568 | tf_op jit(solution)/shard_map/ppermute | solution.py:230
  155.6 11.9 %collective-permute-start.3 = (bf16[64,512]{1,0:T(8,128)(2,1)S(1)}, bf16[64,512]{1,0:T(8,128)(2,1)S(1)}, u32[]{:S(2)}, u32[]{:S(2)}) collective-permute-start(bf16[64,512]{1,0:T(8,128)(2,1)S(1)} %get-tuple-element.19), channel_id=1, source_target_pairs={{0,1},{1,2},{2,3},{3,0},{4,5},{5,6},{6,7},{7,4},{8,9},{9,10},{10,1... | collective-permute-start | bytes 196616 | tf_op jit(solution)/shard_map/ppermute | solution.py:230
  167.5 0.1 collective-permute-done.4.refs_2_
  167.6 1.8 collective-permute-done.3.refs_1_
  169.5 0.6 copy-done.12
  170.0 0.1 copy-done.4
  170.2 0.1 copy-done.5
  170.2 0.1 copy-done.6
  170.3 2.5 shard_map.123
  172.9 0.1 copy.30
  172.9 0.1 eq.47
  173.0 0.1 eq.51
  173.1 1.2 reduce-window.6
  174.4 0.2 slice_reduce_fusion
  174.6 0.2 reduce-window.9
  174.8 0.7 stack.135.source_ref
  175.4 0.7 stack.122.source_ref
  176.1 0.1 add_bitcast_fusion
  176.2 16.9 %shard_map.121.refs_0_ = f32[512,896]{1,0:T(8,128)} custom-call(s32[12]{0:T(128)} %stack.135.source_ref, bf16[512,6144]{1,0:T(8,128)(2,1)} %all-gather.6.cloned.1.call-done.refs_0_, bf16[16384,896]{1,0:T(8,128)(2,1)} %refs_2_.1), custom_call_target="tpu_custom_call" | custom-call | flops 5637144576 | bytes 20971520 | tf_op jit(solution)/shard_map/pallas_call | solution.py:154
  193.1 42.2 %all-gather.8.cloned.1.call-done.refs_1_ = bf16[512,10240]{1,0:T(8,128)(2,1)} async-done(((bf16[64,10240]{1,0:T(8,128)(2,1)}), bf16[512,10240]{1,0:T(8,128)(2,1)}) %all-gather.8.cloned.1.call-update) | async-done | bytes 10485776 | tf_op jit(solution)/shard_map/all_gather | solution.py:236
  235.3 26.3 %shard_map.124 = bf16[512,896]{1,0:T(8,128)(2,1)} custom-call(s32[20]{0:T(128)} %stack.122.source_ref, f32[512,896]{1,0:T(8,128)} %shard_map.121.refs_0_, bf16[512,10240]{1,0:T(8,128)(2,1)} %all-gather.8.cloned.1.call-done.refs_1_, bf16[16384,896]{1,0:T(8,128)(2,1)} %refs_2_.1), custom_call_target="tpu_custom_call" | custom-call | flops 9395240960 | bytes 32505856 | tf_op jit(solution)/shard_map/pallas_call | solution.py:154
  261.6 3.6 %all-to-all-start = ((bf16[8,64,896]{2,1,0:T(8,128)(2,1)}), bf16[8,64,896]{2,1,0:T(8,128)(2,1)S(1)}, u32[]{:S(2)}, u32[]{:S(2)}) async-start(bf16[8,64,896]{2,1,0:T(8,128)(2,1)} %bitcast.97), calls=%async_computation | async-start | bytes 1835008 | tf_op jit(solution)/shard_map/all_to_all | solution.py:246
  265.2 0.1 copy.32
  265.3 0.2 convert_element_type.78
  265.4 0.2 fusion.34
  265.7 13.4 %all-to-all-done = bf16[8,64,896]{2,1,0:T(8,128)(2,1)S(1)} async-done(((bf16[8,64,896]{2,1,0:T(8,128)(2,1)}), bf16[8,64,896]{2,1,0:T(8,128)(2,1)S(1)}, u32[]{:S(2)}, u32[]{:S(2)}) %all-to-all-start) | async-done | bytes 917536 | tf_op jit(solution)/shard_map/all_to_all | solution.py:246
  279.1 0.1 fusion.35
  279.2 0.1 copy.33
  279.4 0.4 fusion.7
  279.8 0.3 copy-done.15
  280.1 0.4 convolution_convert_fusion.1
  280.5 0.1 reshape.109
  280.5 10.3 %all_to_all.24 = bf16[4,2,7168]{2,1,0:T(2,128)(2,1)S(1)} all-to-all(bf16[4,2,7168]{2,1,0:T(2,128)(2,1)S(1)} %reshape.109), channel_id=1, replica_groups=mesh['ctx'=8,'ep'=4] {'ep'}, dimensions={0} | all-to-all | bytes 229376 | tf_op jit(solution)/shard_map/all_to_all | solution.py:270
  290.8 10.0 %all_gather.15 = bf16[32,2,7168]{2,1,0:T(2,128)(2,1)S(1)} all-gather(bf16[4,2,7168]{2,1,0:T(2,128)(2,1)S(1)} %all_to_all.24), channel_id=1, replica_groups=mesh['ctx'=8,'ep'=4] {'ctx'}, dimensions={0}, use_global_device_ids=true | all-gather | bytes 1032192 | tf_op jit(solution)/shard_map/all_gather | solution.py:275
  300.8 0.3 reshape.110
  301.1 2.8 fusion.5
  303.9 5.5 %fusion.1 = bf16[8,8,7168]{2,1,0:T(8,128)(2,1)S(1)} fusion(bf16[1,256,7168]{2,1,0:T(8,128)(2,1)} %param.21, bf16[64,7168]{1,0:T(8,128)(2,1)S(1)} %reshape.110, bf16[1,7168,256]{2,1,0:T(8,128)(2,1)} %param.20, f32[64,256]{1,0:T(8,128)S(1)} %fusion.5), kind=kOutput, calls=%fused_computation.3 | convolution fusion | flops 470319104 | bytes 9240576 | tf_op jit(solution)/shard_map/dot_general | solution.py:281
  309.3 16.5 %all_to_all.25 = bf16[8,8,7168]{2,1,0:T(8,128)(2,1)S(1)} all-to-all(bf16[8,8,7168]{2,1,0:T(8,128)(2,1)S(1)} %fusion.1), channel_id=1, replica_groups=mesh['ctx'=8,'ep'=4] {'ctx'}, dimensions={0} | all-to-all | bytes 1835008 | tf_op jit(solution)/shard_map/all_to_all | solution.py:283
  325.9 0.1 reduce_sum.52
  326.0 8.4 %all_to_all.26 = bf16[4,2,7168]{2,1,0:T(2,128)(2,1)S(1)} all-to-all(bf16[4,2,7168]{2,1,0:T(2,128)(2,1)S(1)} %reshape.112), channel_id=1, replica_groups=mesh['ctx'=8,'ep'=4] {'ep'}, dimensions={0} | all-to-all | bytes 229376 | tf_op jit(solution)/shard_map/all_to_all | solution.py:286
  334.5 1.9 fusion
  (42 shorter events, 0.2 us)
Async XLA Ops:
  6.5 34.8 %all-gather.4.cloned.1.call-start = ((), (), s32[]{:S(2)}) async-start(), calls=%async_computation.4 | async-start | bytes 2654208 | tf_op jit(solution)/shard_map/all_gather | solution.py:200
  7.3 169.0 %all-gather.6.cloned.1.call-start = ((), (), s32[]{:S(2)}) async-start(), calls=%async_computation.5 | async-start | bytes 7077888 | tf_op jit(solution)/shard_map/all_gather | solution.py:236
  41.3 4.5 %copy-start = (bf16[2048,576]{0,1:T(8,128)(2,1)S(1)}, bf16[2048,576]{0,1:T(8,128)(2,1)}, u32[]{:S(2)}) copy-start(bf16[2048,576]{0,1:T(8,128)(2,1)} %all-gather.4.cloned.1.call-done) | copy-start | bytes 7077892
  75.0 16.0 %collective-permute-start.2 = (bf16[64,1536]{1,0:T(8,128)(2,1)S(1)}, bf16[64,1536]{1,0:T(8,128)(2,1)S(1)}, u32[]{:S(2)}, u32[]{:S(2)}) collective-permute-start(bf16[64,1536]{1,0:T(8,128)(2,1)S(1)} %get-tuple-element.13), channel_id=1, source_target_pairs={{0,3},{1,0},{2,1},{3,2},{4,7},{5,4},{6,5},{7,6},{8,11},{9,8},{10,9... | collective-permute-start | bytes 589832 | tf_op jit(solution)/shard_map/ppermute | solution.py:230
  78.3 17.3 %collective-permute-start.1 = (bf16[64,1536]{1,0:T(8,128)(2,1)S(1)}, bf16[64,1536]{1,0:T(8,128)(2,1)S(1)}, u32[]{:S(2)}, u32[]{:S(2)}) collective-permute-start(bf16[64,1536]{1,0:T(8,128)(2,1)S(1)} %get-tuple-element.14), channel_id=1, source_target_pairs={{0,2},{1,3},{2,0},{3,1},{4,6},{5,7},{6,4},{7,5},{8,10},{9,11},{10,... | collective-permute-start | bytes 589832 | tf_op jit(solution)/shard_map/ppermute | solution.py:230
  78.3 17.3 %collective-permute-start = (bf16[64,1536]{1,0:T(8,128)(2,1)S(1)}, bf16[64,1536]{1,0:T(8,128)(2,1)S(1)}, u32[]{:S(2)}, u32[]{:S(2)}) collective-permute-start(bf16[64,1536]{1,0:T(8,128)(2,1)S(1)} %get-tuple-element.15), channel_id=1, source_target_pairs={{0,1},{1,2},{2,3},{3,0},{4,5},{5,6},{6,7},{7,4},{8,9},{9,10},{10,1... | collective-permute-start | bytes 589832 | tf_op jit(solution)/shard_map/ppermute | solution.py:230
  90.2 0.7 copy-start.1
  91.0 4.6 %copy-start.7 = (bf16[64,1536]{1,0:T(8,128)(2,1)}, bf16[64,1536]{1,0:T(8,128)(2,1)S(1)}, u32[]{:S(2)}) copy-start(bf16[64,1536]{1,0:T(8,128)(2,1)S(1)} %collective-permute-done.2.refs_3_) | copy-start | bytes 589828
  95.6 0.7 copy-start.8
  95.6 0.7 copy-start.9
  98.5 42.8 %copy-start.2 = (bf16[256,512]{1,0:T(8,128)(2,1)S(1)}, bf16[256,512]{1,0:T(8,128)(2,1)}, u32[]{:S(2)}) copy-start(bf16[256,512]{1,0:T(8,128)(2,1)} %copy-done.1) | copy-start | bytes 786436
  98.5 136.8 %all-gather.8.cloned.1.call-start = ((), (), s32[]{:S(2)}) async-start(), calls=%async_computation.6 | async-start | bytes 11796480 | tf_op jit(solution)/shard_map/all_gather | solution.py:236
  136.7 36.2 %copy-start.13 = (s32[64,8]{0,1:T(8,128)S(1)}, s32[64,8]{0,1:T(8,128)}, u32[]{:S(2)}) copy-start(s32[64,8]{0,1:T(8,128)} %param.22) | copy-start | bytes 6148
  136.7 32.7 %collective-permute-start.8 = (bf16[64,2048]{1,0:T(8,128)(2,1)S(1)}, bf16[64,2048]{1,0:T(8,128)(2,1)S(1)}, u32[]{:S(2)}, u32[]{:S(2)}) collective-permute-start(bf16[64,2048]{1,0:T(8,128)(2,1)S(1)} %get-tuple-element.9), channel_id=1, source_target_pairs={{0,3},{1,0},{2,1},{3,2},{4,7},{5,4},{6,5},{7,6},{8,11},{9,8},{10,9... | collective-permute-start | bytes 786440 | tf_op jit(solution)/shard_map/ppermute | solution.py:230
  136.8 32.6 %collective-permute-start.7 = (bf16[64,2048]{1,0:T(8,128)(2,1)S(1)}, bf16[64,2048]{1,0:T(8,128)(2,1)S(1)}, u32[]{:S(2)}, u32[]{:S(2)}) collective-permute-start(bf16[64,2048]{1,0:T(8,128)(2,1)S(1)} %get-tuple-element.10), channel_id=1, source_target_pairs={{0,2},{1,3},{2,0},{3,1},{4,6},{5,7},{6,4},{7,5},{8,10},{9,11},{10,... | collective-permute-start | bytes 786440 | tf_op jit(solution)/shard_map/ppermute | solution.py:230
  139.3 30.1 %collective-permute-start.6 = (bf16[64,2048]{1,0:T(8,128)(2,1)S(1)}, bf16[64,2048]{1,0:T(8,128)(2,1)S(1)}, u32[]{:S(2)}, u32[]{:S(2)}) collective-permute-start(bf16[64,2048]{1,0:T(8,128)(2,1)S(1)} %get-tuple-element.11), channel_id=1, source_target_pairs={{0,1},{1,2},{2,3},{3,0},{4,5},{5,6},{6,7},{7,4},{8,9},{9,10},{10,1... | collective-permute-start | bytes 786440 | tf_op jit(solution)/shard_map/ppermute | solution.py:230
  142.0 13.6 %collective-permute-start.5 = (bf16[64,512]{1,0:T(8,128)(2,1)S(1)}, bf16[64,512]{1,0:T(8,128)(2,1)S(1)}, u32[]{:S(2)}, u32[]{:S(2)}) collective-permute-start(bf16[64,512]{1,0:T(8,128)(2,1)S(1)} %get-tuple-element.17), channel_id=1, source_target_pairs={{0,3},{1,0},{2,1},{3,2},{4,7},{5,4},{6,5},{7,6},{8,11},{9,8},{10,9... | collective-permute-start | bytes 196616 | tf_op jit(solution)/shard_map/ppermute | solution.py:230
  143.8 23.8 %collective-permute-start.4 = (bf16[64,512]{1,0:T(8,128)(2,1)S(1)}, bf16[64,512]{1,0:T(8,128)(2,1)S(1)}, u32[]{:S(2)}, u32[]{:S(2)}) collective-permute-start(bf16[64,512]{1,0:T(8,128)(2,1)S(1)} %get-tuple-element.18), channel_id=1, source_target_pairs={{0,2},{1,3},{2,0},{3,1},{4,6},{5,7},{6,4},{7,5},{8,10},{9,11},{10,... | collective-permute-start | bytes 196616 | tf_op jit(solution)/shard_map/ppermute | solution.py:230
  155.6 13.9 %copy-start.10 = (bf16[64,512]{1,0:T(8,128)(2,1)}, bf16[64,512]{1,0:T(8,128)(2,1)S(1)}, u32[]{:S(2)}) copy-start(bf16[64,512]{1,0:T(8,128)(2,1)S(1)} %collective-permute-done.5.refs_3_) | copy-start | bytes 196612
  155.6 13.8 %collective-permute-start.3 = (bf16[64,512]{1,0:T(8,128)(2,1)S(1)}, bf16[64,512]{1,0:T(8,128)(2,1)S(1)}, u32[]{:S(2)}, u32[]{:S(2)}) collective-permute-start(bf16[64,512]{1,0:T(8,128)(2,1)S(1)} %get-tuple-element.19), channel_id=1, source_target_pairs={{0,1},{1,2},{2,3},{3,0},{4,5},{5,6},{6,7},{7,4},{8,9},{9,10},{10,1... | collective-permute-start | bytes 196616 | tf_op jit(solution)/shard_map/ppermute | solution.py:230
  167.6 1.8 copy-start.11
  169.4 0.6 copy-start.12
  169.4 0.7 copy-start.4
  169.4 0.8 copy-start.5
  169.4 0.9 copy-start.6
  193.1 72.0 %copy-start.14 = (f32[64,8]{0,1:T(8,128)S(1)}, f32[64,8]{0,1:T(8,128)}, u32[]{:S(2)}) copy-start(f32[64,8]{0,1:T(8,128)} %param.23) | copy-start | bytes 6148
  261.6 17.5 %all-to-all-start = ((bf16[8,64,896]{2,1,0:T(8,128)(2,1)}), bf16[8,64,896]{2,1,0:T(8,128)(2,1)S(1)}, u32[]{:S(2)}, u32[]{:S(2)}) async-start(bf16[8,64,896]{2,1,0:T(8,128)(2,1)} %bitcast.97), calls=%async_computation | async-start | bytes 1835008 | tf_op jit(solution)/shard_map/all_to_all | solution.py:246
  265.7 13.7 %copy-start.3 = (bf16[64,7168]{1,0:T(8,128)(2,1)S(1)}, bf16[64,7168]{1,0:T(8,128)(2,1)}, u32[]{:S(2)}) copy-start(bf16[64,7168]{1,0:T(8,128)(2,1)} %param.17) | copy-start | bytes 2752516
  279.3 0.8 copy-start.15
Sparse Core Ops, SparseCore 0:
  9.2 32.0 all-gather.3
  98.6 44.8 all-gather.5
  173.0 62.2 all-gather.7
